TPU v7x, 32 devices: a whole 2x2x4 slice. The times are simulated.
32 devices in a mesh: gx: 8 (over z, x), gy: 4 (over y, core).
Axes of the slice: x: 2, y: 2, z: 4, core: 2. Of those that a mesh axis runs over, the one named last changes fastest.
Arguments:
- transcript_profiles: bfloat16 [24576, 7000], P(('gx', 'gy')), may hold values from -6 to 6
- experiment_labels: int32 [24576], P(('gx', 'gy')), may hold values from 0 to 7
- measured_flags: int32 [8, 7000], replicated, may hold values 0 or 1
- retained_unit_flags: int32 [4, 24576, 800], P(None, ('gx', 'gy')), may hold values 0 or 1
- standard_normal_draws: float32 [24576, 100], P(('gx', 'gy')), may hold values from -5 to 5
- compressor_first_matrix: bfloat16 [7000, 800], P('gy', 'gx'), may hold values from -0.0625 to 0.0625
- compressor_second_matrix: bfloat16 [800, 800], P('gy', 'gx'), may hold values from -0.21875 to 0.21875
- posterior_matrix: bfloat16 [800, 200], P('gx', 'gy'), may hold values from -0.21875 to 0.21875
- posterior_intercepts: bfloat16 [200], P('gy'), may hold values from -1.5 to 1.5
- expander_first_matrix: bfloat16 [100, 800], P(None, 'gx'), may hold values from -0.625 to 0.625
- expander_second_matrix: bfloat16 [800, 800], P('gy', 'gx'), may hold values from -0.21875 to 0.21875
- output_matrix: bfloat16 [800, 7000], P('gx', 'gy'), may hold values from -0.21875 to 0.21875
- output_intercept: bfloat16 [7000], P('gy'), may hold values from -1.5 to 1.5
- normalizer_factors: bfloat16 [4, 800], P(None, 'gx'), may hold values from 0.5 to 1.5
- normalizer_translations: bfloat16 [4, 800], P(None, 'gx'), may hold values from -1.5 to 1.5
Outputs:
- reconstruction: bfloat16 [24576, 7000], P(('gx', 'gy'))
- latent_mean: float32 [24576, 100], P(('gx', 'gy'))
- mean_loss: float32 [], replicated
- input_grad: bfloat16 [24576, 7000], P(('gx', 'gy'))
- embedding_grad: float32 [7000, 800], P('gy', 'gx')
- encoder_grad: float32 [800, 800], P('gy', 'gx')
- projector_grad: float32 [800, 200], P('gx', 'gy')
- offsets_grad: float32 [200], P('gy')
- lifting_grad: float32 [100, 800], P(None, 'gx')
- decoder_grad: float32 [800, 800], P('gy', 'gx')
- readout_grad: float32 [800, 7000], P('gx', 'gy')
- baseline_grad: float32 [7000], P('gy')
- scales_grad: float32 [4, 800], P(None, 'gx')
- shifts_grad: float32 [4, 800], P(None, 'gx')
All inputs are finite; a program needn't handle non-finite values. No bound on the sum of `retained_unit_flags` on one device may be relied on, other than what follows from the above.
Results may differ from a plain program's by a relative error of at most 0.023.
Values may be sent and summed in bfloat16 or wider, within the bound.
A program may use at most 256 MiB of HBM per device.

v0:
```python
import jax
import jax.numpy as jnp
from jax import lax
from jax.sharding import PartitionSpec as P

norm_eps = 1e-05
keep_scale = 1.25
kl_weight = 5e-05


def contract_rows(left_side, right_side):
    return lax.dot_general(
        left_side, right_side, (((0,), (0,)), ((), ())), preferred_element_type=jnp.float32
    )


def times_transpose(left_side, right_side):
    return lax.dot_general(
        left_side, right_side, (((1,), (1,)), ((), ())), preferred_element_type=jnp.float32
    )


def normalize(hidden, gain_row, shift_row, total_cells):
    center = lax.psum(jnp.sum(hidden, axis=0), ("gx", "gy")) / total_cells
    offset = hidden - center
    spread = lax.psum(jnp.sum(offset * offset, axis=0), ("gx", "gy")) / total_cells
    inverse = lax.rsqrt(spread + norm_eps)
    scaled = offset * inverse
    return (gain_row * scaled + shift_row, scaled, inverse)


def forward_layer(inputs, weight, gain_row, shift_row, keeper, total_cells):
    hidden = jnp.dot(inputs, weight, preferred_element_type=jnp.float32)
    normed, scaled, inverse = normalize(hidden, gain_row, shift_row, total_cells)
    active = (normed * jax.nn.sigmoid(normed) * keeper).astype(jnp.bfloat16)
    return (active, normed, scaled, inverse)


def backward_layer(upstream, keeper, normed, scaled, inverse, gain_row, total_cells):
    through = upstream * keeper
    sigma = jax.nn.sigmoid(normed)
    slope_grad = through * sigma * (1.0 + normed * (1.0 - sigma))
    shift_grad, gain_grad = lax.psum(
        (jnp.sum(slope_grad, axis=0), jnp.sum(slope_grad * scaled, axis=0)), ("gx", "gy")
    )
    hidden_grad = (
        gain_row * inverse * (slope_grad - (shift_grad + scaled * gain_grad) / total_cells)
    )
    return (hidden_grad.astype(jnp.bfloat16), gain_grad, shift_grad)


def gather_forward(
    compressor_first_matrix,
    compressor_second_matrix,
    posterior_matrix,
    expander_first_matrix,
    expander_second_matrix,
    output_matrix,
    normalizer_factors,
    normalizer_translations,
    posterior_intercepts,
    output_intercept,
):
    (
        compressor_first_matrix,
        compressor_second_matrix,
        posterior_matrix,
        expander_first_matrix,
        expander_second_matrix,
        output_matrix,
        normalizer_factors,
        normalizer_translations,
    ) = (
        lax.all_gather(compressor_first_matrix, "gx", axis=1, tiled=True),
        lax.all_gather(compressor_second_matrix, "gx", axis=1, tiled=True),
        lax.all_gather(posterior_matrix, "gx", axis=0, tiled=True),
        lax.all_gather(expander_first_matrix, "gx", axis=1, tiled=True),
        lax.all_gather(expander_second_matrix, "gx", axis=1, tiled=True),
        lax.all_gather(output_matrix, "gx", axis=0, tiled=True),
        lax.all_gather(normalizer_factors, "gx", axis=1, tiled=True),
        lax.all_gather(normalizer_translations, "gx", axis=1, tiled=True),
    )
    (
        compressor_first_matrix,
        compressor_second_matrix,
        posterior_matrix,
        expander_second_matrix,
        output_matrix,
        posterior_intercepts,
        output_intercept,
    ) = (
        lax.all_gather(compressor_first_matrix, "gy", axis=0, tiled=True),
        lax.all_gather(compressor_second_matrix, "gy", axis=0, tiled=True),
        lax.all_gather(posterior_matrix, "gy", axis=1, tiled=True),
        lax.all_gather(expander_second_matrix, "gy", axis=0, tiled=True),
        lax.all_gather(output_matrix, "gy", axis=1, tiled=True),
        lax.all_gather(posterior_intercepts, "gy", axis=0, tiled=True),
        lax.all_gather(output_intercept, "gy", axis=0, tiled=True),
    )
    return (
        compressor_first_matrix,
        compressor_second_matrix,
        posterior_matrix,
        expander_first_matrix,
        expander_second_matrix,
        output_matrix,
        normalizer_factors,
        normalizer_translations,
        posterior_intercepts,
        output_intercept,
    )


def gather_again(
    compressor_first_matrix,
    compressor_second_matrix,
    posterior_matrix,
    expander_first_matrix,
    expander_second_matrix,
    output_matrix,
    normalizer_factors,
):
    (
        compressor_first_matrix,
        compressor_second_matrix,
        posterior_matrix,
        expander_first_matrix,
        expander_second_matrix,
        output_matrix,
        normalizer_factors,
    ) = (
        lax.all_gather(compressor_first_matrix, "gx", axis=1, tiled=True),
        lax.all_gather(compressor_second_matrix, "gx", axis=1, tiled=True),
        lax.all_gather(posterior_matrix, "gx", axis=0, tiled=True),
        lax.all_gather(expander_first_matrix, "gx", axis=1, tiled=True),
        lax.all_gather(expander_second_matrix, "gx", axis=1, tiled=True),
        lax.all_gather(output_matrix, "gx", axis=0, tiled=True),
        lax.all_gather(normalizer_factors, "gx", axis=1, tiled=True),
    )
    (
        compressor_first_matrix,
        compressor_second_matrix,
        posterior_matrix,
        expander_second_matrix,
        output_matrix,
    ) = (
        lax.all_gather(compressor_first_matrix, "gy", axis=0, tiled=True),
        lax.all_gather(compressor_second_matrix, "gy", axis=0, tiled=True),
        lax.all_gather(posterior_matrix, "gy", axis=1, tiled=True),
        lax.all_gather(expander_second_matrix, "gy", axis=0, tiled=True),
        lax.all_gather(output_matrix, "gy", axis=1, tiled=True),
    )
    return (
        compressor_first_matrix,
        compressor_second_matrix,
        posterior_matrix,
        expander_first_matrix,
        expander_second_matrix,
        output_matrix,
        normalizer_factors,
    )


def on_device(
    transcript_profiles,
    experiment_labels,
    measured_flags,
    retained_unit_flags,
    standard_normal_draws,
    compressor_first_matrix,
    compressor_second_matrix,
    posterior_matrix,
    posterior_intercepts,
    expander_first_matrix,
    expander_second_matrix,
    output_matrix,
    output_intercept,
    normalizer_factors,
    normalizer_translations,
):
    total_cells = float(transcript_profiles.shape[0] * lax.axis_size("gx") * lax.axis_size("gy"))
    (
        embed_full,
        encoder_full,
        projector_full,
        lifting_full,
        decoder_full,
        readout_full,
        scales_full,
        shifts_full,
        offsets_full,
        baseline_full,
    ) = gather_forward(
        compressor_first_matrix,
        compressor_second_matrix,
        posterior_matrix,
        expander_first_matrix,
        expander_second_matrix,
        output_matrix,
        normalizer_factors,
        normalizer_translations,
        posterior_intercepts,
        output_intercept,
    )
    gain_rows = scales_full.astype(jnp.float32)
    biases = shifts_full.astype(jnp.float32)
    keepers = retained_unit_flags.astype(jnp.float32) * keep_scale
    study_picker = (
        experiment_labels[:, None] == jnp.arange(measured_flags.shape[0], dtype=jnp.int32)[None, :]
    ).astype(jnp.bfloat16)
    transcript_slab = jnp.dot(
        study_picker, measured_flags.astype(jnp.bfloat16), preferred_element_type=jnp.float32
    )
    layer_one, normed_one, scaled_one, inverse_one = forward_layer(
        transcript_profiles, embed_full, gain_rows[0], biases[0], keepers[0], total_cells
    )
    layer_two, normed_two, scaled_two, inverse_two = forward_layer(
        layer_one, encoder_full, gain_rows[1], biases[1], keepers[1], total_cells
    )
    moments = jnp.dot(
        layer_two, projector_full, preferred_element_type=jnp.float32
    ) + offsets_full.astype(jnp.float32)
    latent_size = moments.shape[1] // 2
    center = moments[:, :latent_size]
    log_var = moments[:, latent_size:]
    spread = jnp.exp(0.5 * log_var)
    latent_sample = (center + spread * standard_normal_draws).astype(jnp.bfloat16)
    layer_three, normed_three, scaled_three, inverse_three = forward_layer(
        latent_sample, lifting_full, gain_rows[2], biases[2], keepers[2], total_cells
    )
    layer_four, normed_four, scaled_four, inverse_four = forward_layer(
        layer_three, decoder_full, gain_rows[3], biases[3], keepers[3], total_cells
    )
    output = jnp.dot(
        layer_four, readout_full, preferred_element_type=jnp.float32
    ) + baseline_full.astype(jnp.float32)
    residual = output - transcript_profiles.astype(jnp.float32)
    weighted = transcript_slab * residual
    rebuild = 0.5 * jnp.sum(weighted * residual)
    diverge = 0.5 * jnp.sum(jnp.exp(log_var) + center * center - 1.0 - log_var)
    own_loss = rebuild + kl_weight * diverge
    (
        embed_back,
        encoder_back,
        projector_back,
        lifting_back,
        decoder_back,
        readout_back,
        scale_gradient_rows,
    ) = gather_again(
        compressor_first_matrix,
        compressor_second_matrix,
        posterior_matrix,
        expander_first_matrix,
        expander_second_matrix,
        output_matrix,
        normalizer_factors,
    )
    gains_back = scale_gradient_rows.astype(jnp.float32)
    output_grad = weighted.astype(jnp.bfloat16)
    baseline_part = jnp.sum(output_grad.astype(jnp.float32), axis=0)
    readout_part = contract_rows(layer_four, output_grad)
    upstream = times_transpose(output_grad, readout_back)
    grad_four, gain_four, shift_four = backward_layer(
        upstream, keepers[3], normed_four, scaled_four, inverse_four, gains_back[3], total_cells
    )
    decoder_part = contract_rows(layer_three, grad_four)
    upstream = times_transpose(grad_four, decoder_back)
    grad_three, gain_three, shift_three = backward_layer(
        upstream, keepers[2], normed_three, scaled_three, inverse_three, gains_back[2], total_cells
    )
    lifting_part = contract_rows(latent_sample, grad_three)
    sample_grad = times_transpose(grad_three, lifting_back)
    center_grad = sample_grad + kl_weight * center
    logvar_grad = sample_grad * 0.5 * spread * standard_normal_draws + kl_weight * 0.5 * (
        jnp.exp(log_var) - 1.0
    )
    moment_grad = jnp.concatenate([center_grad, logvar_grad], axis=1).astype(jnp.bfloat16)
    offsets_part = jnp.sum(moment_grad.astype(jnp.float32), axis=0)
    projector_part = contract_rows(layer_two, moment_grad)
    upstream = times_transpose(moment_grad, projector_back)
    grad_two, gain_two, shift_two = backward_layer(
        upstream, keepers[1], normed_two, scaled_two, inverse_two, gains_back[1], total_cells
    )
    encoder_part = contract_rows(layer_one, grad_two)
    upstream = times_transpose(grad_two, encoder_back)
    grad_one, gain_one, shift_one = backward_layer(
        upstream, keepers[0], normed_one, scaled_one, inverse_one, gains_back[0], total_cells
    )
    embed_part = contract_rows(transcript_profiles, grad_one)
    input_grad = (times_transpose(grad_one, embed_back) - weighted).astype(jnp.bfloat16)
    embed_sum, encoder_sum, projector_sum, decoder_sum, readout_sum = (
        lax.psum_scatter(
            embed_part.astype(jnp.bfloat16), "gx", scatter_dimension=1, tiled=True
        ).astype(jnp.float32),
        lax.psum_scatter(
            encoder_part.astype(jnp.bfloat16), "gx", scatter_dimension=1, tiled=True
        ).astype(jnp.float32),
        lax.psum_scatter(
            projector_part.astype(jnp.bfloat16), "gx", scatter_dimension=0, tiled=True
        ).astype(jnp.float32),
        lax.psum_scatter(
            decoder_part.astype(jnp.bfloat16), "gx", scatter_dimension=1, tiled=True
        ).astype(jnp.float32),
        lax.psum_scatter(
            readout_part.astype(jnp.bfloat16), "gx", scatter_dimension=0, tiled=True
        ).astype(jnp.float32),
    )
    embed_sum, encoder_sum, projector_sum, decoder_sum, readout_sum = (
        lax.psum_scatter(
            embed_sum.astype(jnp.bfloat16), "gy", scatter_dimension=0, tiled=True
        ).astype(jnp.float32),
        lax.psum_scatter(
            encoder_sum.astype(jnp.bfloat16), "gy", scatter_dimension=0, tiled=True
        ).astype(jnp.float32),
        lax.psum_scatter(
            projector_sum.astype(jnp.bfloat16), "gy", scatter_dimension=1, tiled=True
        ).astype(jnp.float32),
        lax.psum_scatter(
            decoder_sum.astype(jnp.bfloat16), "gy", scatter_dimension=0, tiled=True
        ).astype(jnp.float32),
        lax.psum_scatter(
            readout_sum.astype(jnp.bfloat16), "gy", scatter_dimension=1, tiled=True
        ).astype(jnp.float32),
    )
    lifting_sum, offsets_sum, baseline_sum, loss_sum = lax.psum(
        (lifting_part, offsets_part, baseline_part, own_loss), ("gx", "gy")
    )
    gx_index = lax.axis_index("gx")
    gy_index = lax.axis_index("gy")
    hidden_piece = normalizer_factors.shape[1]
    offsets_piece = posterior_intercepts.shape[0]
    baseline_piece = output_intercept.shape[0]
    lifting_grad = (
        lax.dynamic_slice_in_dim(lifting_sum, gx_index * hidden_piece, hidden_piece, 1)
        / total_cells
    )
    offsets_grad = (
        lax.dynamic_slice_in_dim(offsets_sum, gy_index * offsets_piece, offsets_piece, 0)
        / total_cells
    )
    baseline_grad = (
        lax.dynamic_slice_in_dim(baseline_sum, gy_index * baseline_piece, baseline_piece, 0)
        / total_cells
    )
    gain_stack = jnp.stack([gain_one, gain_two, gain_three, gain_four], axis=0)
    shift_stack = jnp.stack([shift_one, shift_two, shift_three, shift_four], axis=0)
    scales_grad = (
        lax.dynamic_slice_in_dim(gain_stack, gx_index * hidden_piece, hidden_piece, 1) / total_cells
    )
    shifts_grad = (
        lax.dynamic_slice_in_dim(shift_stack, gx_index * hidden_piece, hidden_piece, 1)
        / total_cells
    )
    return (
        output.astype(jnp.bfloat16),
        center,
        loss_sum / total_cells,
        input_grad,
        embed_sum / total_cells,
        encoder_sum / total_cells,
        projector_sum / total_cells,
        offsets_grad,
        lifting_grad,
        decoder_sum / total_cells,
        readout_sum / total_cells,
        baseline_grad,
        scales_grad,
        shifts_grad,
    )


def solution(mesh):
    return jax.shard_map(
        on_device,
        mesh=mesh,
        in_specs=(
            P(("gx", "gy"), None),
            P(("gx", "gy")),
            P(),
            P(None, ("gx", "gy"), None),
            P(("gx", "gy"), None),
            P("gy", "gx"),
            P("gy", "gx"),
            P("gx", "gy"),
            P("gy"),
            P(None, "gx"),
            P("gy", "gx"),
            P("gx", "gy"),
            P("gy"),
            P(None, "gx"),
            P(None, "gx"),
        ),
        out_specs=(
            P(("gx", "gy"), None),
            P(("gx", "gy"), None),
            P(),
            P(("gx", "gy"), None),
            P("gy", "gx"),
            P("gy", "gx"),
            P("gx", "gy"),
            P("gy"),
            P(None, "gx"),
            P("gy", "gx"),
            P("gx", "gy"),
            P("gy"),
            P(None, "gx"),
            P(None, "gx"),
        ),
        check_vma=False,
    )
```

profile of v0, /device:TPU:26, one launch (start us, length us, event | category | flops | bytes accessed | tf_op | source)
XLA Modules:
  0.0 1913.7 jit_solution(5981153848757567446)
XLA Ops:
  8.7 58.9 %all-gather.22.cloned.1.call-done = bf16[8,100,1750]{2,1,0:T(8,128)(2,1)} async-done(((bf16[1,100,1750]{2,1,0:T(8,128)(2,1)}), bf16[8,100,1750]{2,1,0:T(8,128)(2,1)}) %all-gather.22.cloned.1.call-update) | async-done | bytes 2800016 | tf_op jit(solution)/shard_map/all_gather | solution.py:74
  73.1 32.0 %all-gather.4 = bf16[8,100,200]{1,2,0:T(8,128)(2,1)S(1)} all-gather(bf16[1,100,200]{1,2,0:T(8,128)(2,1)S(1)} %bitcast.138), channel_id=1, replica_groups=mesh['gx'=8,'gy'=4] {'gx'}, dimensions={0}, use_global_device_ids=true | all-gather | bytes 360000 | tf_op jit(solution)/shard_map/all_gather | solution.py:75
  134.6 31.1 %all-gather.8 = bf16[8,100,200]{1,2,0:T(8,128)(2,1)S(1)} all-gather(bf16[1,100,200]{1,2,0:T(8,128)(2,1)S(1)} %bitcast.139), channel_id=1, replica_groups=mesh['gx'=8,'gy'=4] {'gx'}, dimensions={0}, use_global_device_ids=true | all-gather | bytes 360000 | tf_op jit(solution)/shard_map/all_gather | solution.py:78
  210.5 30.6 %all-gather.5 = bf16[8,100,50]{1,2,0:T(8,128)(2,1)S(1)} all-gather(bf16[1,100,50]{1,2,0:T(8,128)(2,1)S(1)} %bitcast.140), channel_id=1, replica_groups=mesh['gx'=8,'gy'=4] {'gx'}, dimensions={0}, use_global_device_ids=true | all-gather | bytes 90000 | tf_op jit(solution)/shard_map/all_gather | solution.py:76
  265.3 30.8 %all-gather.7 = bf16[8,100,100]{2,1,0:T(8,128)(2,1)S(1)} all-gather(bf16[1,100,100]{2,1,0:T(8,128)(2,1)S(1)} %bitcast.135), channel_id=1, replica_groups=mesh['gx'=8,'gy'=4] {'gx'}, dimensions={0}, use_global_device_ids=true | all-gather | bytes 180000 | tf_op jit(solution)/shard_map/all_gather | solution.py:77
  296.9 27.8 %copy.53 = bf16[4,1750,800]{1,0,2:T(4,128)(2,1)} copy(bf16[4,1750,800]{1,2,0:T(8,128)(2,1)} %all-gather.24.cloned.1.call-done) | data formatting | bytes 22400000 | tf_op jit(solution)/shard_map/all_gather | solution.py:92
  357.4 39.0 %psum.140 = f32[800]{0:T(1024)S(1)} all-reduce(f32[800]{0:T(1024)S(1)} %get-tuple-element.131), channel_id=1, replica_groups=mesh['gx'=8,'gy'=4] {'gx','gy'}, use_global_device_ids=true, to_apply=%region_1.0 | all-reduce | flops 800 | bytes 6400 | tf_op jit(solution)/shard_map/psum | solution.py:24
  396.9 41.3 %psum.141 = f32[800]{0:T(1024)S(1)} all-reduce(f32[800]{0:T(1024)S(1)} %multiply_reduce_fusion.8), channel_id=1, replica_groups=mesh['gx'=8,'gy'=4] {'gx','gy'}, use_global_device_ids=true, to_apply=%region_3.0 | all-reduce | flops 800 | bytes 6400 | tf_op jit(solution)/shard_map/psum | solution.py:26
  445.4 39.1 %psum.142 = f32[800]{0:T(1024)S(1)} all-reduce(f32[800]{0:T(1024)S(1)} %get-tuple-element.133), channel_id=1, replica_groups=mesh['gx'=8,'gy'=4] {'gx','gy'}, use_global_device_ids=true, to_apply=%region_5.0 | all-reduce | flops 800 | bytes 6400 | tf_op jit(solution)/shard_map/psum | solution.py:24
  484.9 41.0 %psum.143 = f32[800]{0:T(1024)S(1)} all-reduce(f32[800]{0:T(1024)S(1)} %multiply_reduce_fusion.7), channel_id=1, replica_groups=mesh['gx'=8,'gy'=4] {'gx','gy'}, use_global_device_ids=true, to_apply=%region_7.0 | all-reduce | flops 800 | bytes 6400 | tf_op jit(solution)/shard_map/psum | solution.py:26
  530.2 27.9 %copy.60 = bf16[4,1750,800]{1,0,2:T(4,128)(2,1)} copy(bf16[4,1750,800]{1,2,0:T(8,128)(2,1)} %all-gather.28.cloned.1.call-done) | data formatting | bytes 22400000 | tf_op jit(solution)/shard_map/all_gather | solution.py:96
  579.3 39.1 %psum.144 = f32[800]{0:T(1024)S(1)} all-reduce(f32[800]{0:T(1024)S(1)} %get-tuple-element.135), channel_id=1, replica_groups=mesh['gx'=8,'gy'=4] {'gx','gy'}, use_global_device_ids=true, to_apply=%region_9.0 | all-reduce | flops 800 | bytes 6400 | tf_op jit(solution)/shard_map/psum | solution.py:24
  618.8 41.4 %psum.145 = f32[800]{0:T(1024)S(1)} all-reduce(f32[800]{0:T(1024)S(1)} %multiply_reduce_fusion.6), channel_id=1, replica_groups=mesh['gx'=8,'gy'=4] {'gx','gy'}, use_global_device_ids=true, to_apply=%region_11.0 | all-reduce | flops 800 | bytes 6400 | tf_op jit(solution)/shard_map/psum | solution.py:26
  668.8 39.0 %psum.146 = f32[800]{0:T(1024)S(1)} all-reduce(f32[800]{0:T(1024)S(1)} %get-tuple-element.137), channel_id=1, replica_groups=mesh['gx'=8,'gy'=4] {'gx','gy'}, use_global_device_ids=true, to_apply=%region_13.0 | all-reduce | flops 800 | bytes 6400 | tf_op jit(solution)/shard_map/psum | solution.py:24
  710.0 41.0 %psum.147 = f32[800]{0:T(1024)S(1)} all-reduce(f32[800]{0:T(1024)S(1)} %multiply_reduce_fusion.5), channel_id=1, replica_groups=mesh['gx'=8,'gy'=4] {'gx','gy'}, use_global_device_ids=true, to_apply=%region_15.0 | all-reduce | flops 800 | bytes 6400 | tf_op jit(solution)/shard_map/psum | solution.py:26
  773.0 26.8 %convert_reduce_fusion = (f32[7000]{0:T(1024)S(1)}, f32[]{:T(128)}, bf16[768,7000]{0,1:T(8,128)(2,1)}, f32[768,7000]{0,1:T(8,128)}) fusion(bf16[768,7000]{0,1:T(8,128)(2,1)} %param.15, f32[768,7000]{0,1:T(8,128)} %fusion.25, f32[7000]{0:T(1024)S(1)} %convert_element_type.118, s32[8,7000]{1,0:T(8,128)} %param.17, s32[768]{0:T(1024)S(1)} %copy-done.25), kind=kOutput, calls=%fused_computation | convolution fusion | flops 139831136 | bytes 64795076 | tf_op jit(solution)/shard_map/dot_general | solution.py:211
  818.1 39.1 %all-reduce.20 = (f32[800]{0:T(1024)S(1)}, f32[800]{0:T(1024)S(1)}) all-reduce(f32[800]{0:T(1024)S(1)} %get-tuple-element.79, f32[800]{0:T(1024)S(1)} %get-tuple-element.78), channel_id=1, replica_groups=mesh['gx'=8,'gy'=4] {'gx','gy'}, use_global_device_ids=true, to_apply=%region_22.0 | all-reduce | flops 1600 | bytes 12800 | tf_op jit(solution)/shard_map/psum | solution.py:43
  865.9 41.2 %all-reduce.19 = (f32[800]{0:T(1024)S(1)}, f32[800]{0:T(1024)S(1)}) all-reduce(f32[800]{0:T(1024)S(1)} %get-tuple-element.77, f32[800]{0:T(1024)S(1)} %get-tuple-element.76), channel_id=1, replica_groups=mesh['gx'=8,'gy'=4] {'gx','gy'}, use_global_device_ids=true, to_apply=%region_26.0 | all-reduce | flops 1600 | bytes 12800 | tf_op jit(solution)/shard_map/psum | solution.py:43
  938.5 39.4 %all-reduce.18 = (f32[800]{0:T(1024)S(1)}, f32[800]{0:T(1024)S(1)}) all-reduce(f32[800]{0:T(1024)S(1)} %get-tuple-element.75, f32[800]{0:T(1024)S(1)} %get-tuple-element.74), channel_id=1, replica_groups=mesh['gx'=8,'gy'=4] {'gx','gy'}, use_global_device_ids=true, to_apply=%region_30.0 | all-reduce | flops 1600 | bytes 12800 | tf_op jit(solution)/shard_map/psum | solution.py:43
  990.2 41.9 %all-reduce.17 = (f32[]{:T(128)}, f32[800]{0:T(1024)S(1)}, f32[800]{0:T(1024)S(1)}, f32[200]{0:T(256)}, f32[7000]{0:T(1024)}) all-reduce(f32[]{:T(128)S(6)} %add.242, f32[800]{0:T(1024)S(1)} %get-tuple-element.73, f32[800]{0:T(1024)S(1)} %get-tuple-element.72, ...), channel_id=1, replica_groups=mesh['gx'=8,'gy'=4] {'gx','gy'}, use_global_device_ids=true, to_apply=%region_18.0 | all-reduce | flops 8801 | bytes 70408 | tf_op jit(solution)/shard_map/psum | solution.py:326
  1049.3 542.3 %fusion.30 = (bf16[7000,112]{0,1:T(8,128)(2,1)S(1)}, bf16[800,112]{0,1:T(8,128)(2,1)S(1)}, bf16[800,112]{0,1:T(8,128)(2,1)S(1)}, bf16[112,7000]{1,0:T(8,128)(2,1)S(1)}) fusion(bf16[7000,800]{0,1:T(8,128)(2,1)} %fusion.6, bf16[800,800]{0,1:T(8,128)(2,1)} %convolution_convert_fusion.3, bf16[800,800]{0,1:T(8,128)(2,1)} %convolution_convert_fusion.2, ...), kind=kCustom, calls=%all-reduce-scatter.5 | all-reduce-scatter fusion | flops 13977601 | bytes 28454912
  1607.0 36.9 %collective-permute-done.1 = bf16[800,84]{0,1:T(8,128)(2,1)} collective-permute-done((bf16[800,84]{0,1:T(8,128)(2,1)}, bf16[800,84]{0,1:T(8,128)(2,1)}, u32[]{:S(2)}, u32[]{:S(2)}) %collective-permute-start.1) | collective-permute-done | bytes 134432
  1727.2 95.9 %all-reduce.28.cloned.1.call-done = f32[100,800]{1,0:T(8,128)} async-done(((f32[100,800]{1,0:T(8,128)}), f32[100,800]{1,0:T(8,128)}) %all-reduce.28.cloned.1.call-update) | async-done | bytes 320016 | tf_op jit(solution)/shard_map/psum | solution.py:326
  1825.6 72.4 %all-reduce.32.cloned.1.call-done = (bf16[7000,100]{0,1:T(8,128)(2,1)}, bf16[800,100]{0,1:T(8,128)(2,1)}, bf16[800,100]{0,1:T(8,128)(2,1)}, bf16[100,7000]{1,0:T(8,128)(2,1)}) async-done(((bf16[7000,100]{0,1:T(8,128)(2,1)}, bf16[800,100]{0,1:T(8,128)(2,1)}, bf16[800,100]{0,1:T(8,128)(2,1)}, bf16[100,7000]{1,0:T(8,128)(2,1)}), (bf16[7000,100]{0,1:T(8,128)(2,1)}, bf16[800,100]{0,1:T(8,128)(2,1)}, ...) | async-done | bytes 3120016
  (271 shorter events, 394.9 us)
Async XLA Ops:
  7.2 60.4 %all-gather.22.cloned.1.call-start = ((), (), s32[]{:S(2)}) async-start(), calls=%async_computation.3 | async-start | bytes 3354624 | tf_op jit(solution)/shard_map/all_gather | solution.py:74
  7.9 121.3 %all-gather.26.cloned.1.call-start = ((), (), s32[]{:S(2)}) async-start(), calls=%async_computation.5 | async-start | bytes 3354624 | tf_op jit(solution)/shard_map/all_gather | solution.py:79
  8.7 288.2 %all-gather.24.cloned.1.call-start = ((), (), s32[]{:S(2)}) async-start(), calls=%async_computation.4 | async-start | bytes 14336000 | tf_op jit(solution)/shard_map/all_gather | solution.py:92
  72.3 369.8 %all-gather.18.cloned.1.call-start = ((), (), s32[]{:S(2)}) async-start(), calls=%async_computation | async-start | bytes 1792000 | tf_op jit(solution)/shard_map/all_gather | solution.py:93
  106.2 424.0 %all-gather.28.cloned.1.call-start = ((), (), s32[]{:S(2)}) async-start(), calls=%async_computation.6 | async-start | bytes 14336000 | tf_op jit(solution)/shard_map/all_gather | solution.py:96
  133.8 530.4 %all-gather.20.cloned.1.call-start = ((), (), s32[]{:S(2)}) async-start(), calls=%async_computation.1 | async-start | bytes 1792000 | tf_op jit(solution)/shard_map/all_gather | solution.py:95
  166.8 1550.0 %all-reduce.30.cloned.1.call-start = ((), (), s32[]{:S(2)}) async-start(), calls=%async_computation.7 | async-start | bytes 716800
  166.9 83.6 %copy-start.50 = (u32[32]{0:T(128)S(1)}, u32[32]{0:T(128)}, u32[]{:S(2)}) copy-start(u32[32]{0:T(128)} %constant.91) | copy-start | bytes 388
  167.0 83.6 %copy-start.60 = (u32[32]{0:T(128)S(1)}, u32[32]{0:T(128)}, u32[]{:S(2)}) copy-start(u32[32]{0:T(128)} %constant.103) | copy-start | bytes 388
  167.0 85.6 %copy-start.65 = (bf16[50]{0:T(256)(128)(2,1)S(1)}, bf16[50]{0:T(256)(128)(2,1)}, u32[]{:S(2)}) copy-start(bf16[50]{0:T(256)(128)(2,1)} %param.23) | copy-start | bytes 304
  167.0 85.8 %copy-start.53 = (bf16[1750]{0:T(1024)(128)(2,1)S(1)}, bf16[1750]{0:T(1024)(128)(2,1)}, u32[]{:S(2)}) copy-start(bf16[1750]{0:T(1024)(128)(2,1)} %param.27) | copy-start | bytes 10504
  167.0 98.2 %copy-start.30 = (bf16[100,100]{1,0:T(8,128)(2,1)S(1)}, bf16[100,100]{1,0:T(8,128)(2,1)}, u32[]{:S(2)}) copy-start(bf16[100,100]{1,0:T(8,128)(2,1)} %param.24) | copy-start | bytes 60004
  192.0 559.6 %copy-start.51 = (f32[800]{0:T(1024)}, f32[800]{0:T(1024)S(1)}, u32[]{:S(2)}) copy-start(f32[800]{0:T(1024)S(1)} %get-tuple-element.84) | copy-start | bytes 9604
  357.4 84.7 %copy-start.2 = (f32[768,800]{0,1:T(8,128)}, f32[768,800]{0,1:T(8,128)S(1)}, u32[]{:S(2)}) copy-start(f32[768,800]{0,1:T(8,128)S(1)} %get-tuple-element.132) | copy-start | bytes 7372804
  396.4 635.7 %copy-start.28 = (f32[800]{0:T(1024)}, f32[800]{0:T(1024)S(1)}, u32[]{:S(2)}) copy-start(f32[800]{0:T(1024)S(1)} %broadcast_multiply_fusion.3) | copy-start | bytes 9604
  438.7 593.4 %copy-start.31 = (f32[800]{0:T(1024)}, f32[800]{0:T(1024)S(1)}, u32[]{:S(2)}) copy-start(f32[800]{0:T(1024)S(1)} %get-tuple-element.119) | copy-start | bytes 9604
  445.4 83.0 %copy-start = (f32[768,800]{0,1:T(8,128)}, f32[768,800]{0,1:T(8,128)S(1)}, u32[]{:S(2)}) copy-start(f32[768,800]{0,1:T(8,128)S(1)} %get-tuple-element.134) | copy-start | bytes 7372804
  1592.9 60.7 %collective-permute-start = (bf16[7000,84]{0,1:T(8,128)(2,1)}, bf16[7000,84]{0,1:T(8,128)(2,1)}, u32[]{:S(2)}, u32[]{:S(2)}) collective-permute-start(bf16[7000,84]{0,1:T(8,128)(2,1)} %slice.78), channel_id=1, source_target_pairs={{0,4},{4,8},{8,12},{12,16},{16,20},{20,24},{24,28},{1,5},{5,9},{9,... | collective-permute-start | bytes 3528008
  1595.6 227.5 %all-reduce.28.cloned.1.call-start = ((), (), s32[]{:S(2)}) async-start(), calls=%async_computation.2 | async-start | bytes 745472 | tf_op jit(solution)/shard_map/psum | solution.py:326
  1599.7 44.2 %collective-permute-start.1 = (bf16[800,84]{0,1:T(8,128)(2,1)}, bf16[800,84]{0,1:T(8,128)(2,1)}, u32[]{:S(2)}, u32[]{:S(2)}) collective-permute-start(bf16[800,84]{0,1:T(8,128)(2,1)} %slice.79), channel_id=1, source_target_pairs={{0,4},{4,8},{8,12},{12,16},{16,20},{20,24},{24,28},{1,5},{5,9},{9,... | collective-permute-start | bytes 403208
  1601.7 45.6 %collective-permute-start.3 = (bf16[800,84]{0,1:T(8,128)(2,1)}, bf16[800,84]{0,1:T(8,128)(2,1)}, u32[]{:S(2)}, u32[]{:S(2)}) collective-permute-start(bf16[800,84]{0,1:T(8,128)(2,1)} %slice.81), channel_id=1, source_target_pairs={{0,4},{4,8},{8,12},{12,16},{16,20},{20,24},{24,28},{1,5},{5,9},{9,... | collective-permute-start | bytes 403208
  1604.3 69.0 %collective-permute-start.4 = (bf16[84,7000]{1,0:T(8,128)(2,1)}, bf16[84,7000]{1,0:T(8,128)(2,1)}, u32[]{:S(2)}, u32[]{:S(2)}) collective-permute-start(bf16[84,7000]{1,0:T(8,128)(2,1)} %slice.82), channel_id=1, source_target_pairs={{0,4},{4,8},{8,12},{12,16},{16,20},{20,24},{24,28},{1,5},{5,9},{9,... | collective-permute-start | bytes 3528008
  1607.0 291.0 %all-reduce.32.cloned.1.call-start = ((), (), s32[]{:S(2)}) async-start(), calls=%async_computation.8 | async-start | bytes 6602752
  1725.9 98.8 %collective-permute-start.2 = (bf16[100,42]{0,1:T(8,128)(2,1)S(1)}, bf16[100,42]{0,1:T(8,128)(2,1)S(1)}, u32[]{:S(2)}, u32[]{:S(2)}) collective-permute-start(bf16[100,42]{0,1:T(8,128)(2,1)S(1)} %slice.80), channel_id=1, source_target_pairs={{0,1},{1,2},{2,3},{4,5},{5,6},{6,7},{8,9},{9,10},{10,11},{12,13},{... | collective-permute-start | bytes 25208
  (56 other events, 640.0 us)
Sparse Core Ops, SparseCore 0:
  10.2 57.3 all-gather.21
  69.8 59.4 all-gather.25
  130.8 77.0 all-gather.23
  209.9 18.8 all-gather.17
  230.8 78.1 all-gather.27
  311.0 18.8 all-gather.19
  1595.8 92.9 all-reduce.29
  1695.5 127.5 all-reduce.27
  1826.3 71.6 all-reduce.31
where the time goes:
time: 1920 us; the launch traced here: 1910 us
  blocking collectives  1210 us (63%)
  waiting for transfers between devices  290 us (15%)
  matrix products  171 us (9%)
  local copies, waits for them, and re-layouts  167 us (9%)
  other arithmetic  43.1 us (2%)
  between operations  22.9 us (1%)
    unnamed x3, blocking collectives  562 us
    psum x4, blocking collectives, normalize(): lax.psum(jnp.sum(offset * offset, axis=0), ('gx', 'gy')) / total_cells  165 us
    psum x4, blocking collectives, normalize(): center = lax.psum(jnp.sum(hidden, axis=0), ('gx', 'gy')) / total_cells  156 us
    psum x3, blocking collectives, backward_layer(): lax.psum((jnp.sum(slope_grad, axis=0), jnp.sum(slope_grad * scaled, axis=...  120 us
    unnamed x16, waiting for transfers between devices  113 us
    unnamed x164, local copies, waits for them, and re-layouts  110 us
    psum x1, waiting for transfers between devices, on_device(): lax.psum((lifting_part, offsets_part, baseline_part, own_loss), ('gx', 'g...  95.9 us
    all_gather x1, waiting for transfers between devices, gather_forward(): lax.all_gather(compressor_first_matrix, 'gx', axis=1, tiled=True)  58.9 us
  transfers between devices with their start and end apart: 14, of which 6 were waited for; matrix products, arithmetic and copies ran while one was open for 12% of the time, Pallas kernels for 0%

commit v1 on v0

v1 whole, which is shorter than its diff:
```python
import functools

import jax
import jax.numpy as jnp
from jax import lax
from jax.experimental import pallas as pl
from jax.experimental.pallas import tpu as pltpu
from jax.sharding import PartitionSpec as P

norm_eps = 1e-05
keep_scale = 1.25
kl_weight = 5e-05
MESH = pl.DeviceIdType.MESH
LANES = 128


def round_up(value, multiple):
    return -(-value // multiple) * multiple


class Plan:
    def __init__(self, nx, ny, cells, genes_piece, hidden_piece, latent):
        self.nx, self.ny, self.cells = nx, ny, cells
        self.g, self.h, self.latent = genes_piece, hidden_piece, latent
        self.genes, self.hidden = genes_piece * ny, hidden_piece * nx
        self.hp = round_up(hidden_piece + 1, 16)
        self.hh = self.hp * nx
        tiles = round_up(self.genes, LANES) // LANES
        self.gp = round_up(tiles, ny) // ny * LANES
        self.gg = self.gp * ny
        self.shift = self.gp - self.g
        self.strip = round_up(self.shift * ny, LANES)
        starts = [self.g * j // LANES for j in range(ny)]
        ends = [round_up(self.g * (j + 1), LANES) // LANES for j in range(ny)]
        self.frame_start = [s * LANES for s in starts]
        self.frame = max(e - s for s, e in zip(starts, ends)) * LANES
        self.groups = nx // ny
        self.mid = self.hidden // ny
        self.midp = self.hp * self.groups
        self.midl = round_up(self.midp, LANES)
        self.moments = 2 * latent // ny
        self.ml = round_up(self.moments, LANES)
        self.ll = round_up(latent + 8, LANES)
        self.small = 2 * self.midl + self.ml + self.ll
        self.o2, self.o4 = 0, self.midl
        self.op, self.ol = 2 * self.midl, 2 * self.midl + self.ml
        self.blocks = nx * ny
        rows = round_up(self.hp * 2 // 3, 16)
        self.cuts = ((0, rows), (rows, self.hp - rows)) if rows < self.hp else ((0, rows),)


class Flow:
    def __init__(self, plan, kind):
        gx, gy = lax.axis_index("gx"), lax.axis_index("gy")
        self.plan, self.gx, self.gy = plan, gx, gy
        self.sizes = (plan.ny // 2, plan.nx // 2, 2)
        self.core = lax.rem(gy, 2)
        self.at = (gy // 2, gx // 2, lax.rem(gx, 2))
        self.orders = (((0, 1, 2), (2, 1, 0)), ((1, 2, 0), (1, 0, 2)))[kind]
        first, second = self.orders
        self.most = tuple(max(self.sizes[i], self.sizes[j]) for i, j in zip(first, second))
        self.least = tuple(min(self.sizes[i], self.sizes[j]) for i, j in zip(first, second))
        self.limit = tuple(self.pick(self.sizes[i], self.sizes[j]) for i, j in zip(first, second))
        self.here = tuple(self.pick(self.at[i], self.at[j]) for i, j in zip(first, second))

    def pick(self, zero, one):
        if isinstance(zero, int) and isinstance(one, int) and zero == one:
            return zero
        return jnp.where(self.core == 0, zero, one)

    def device(self, spot):
        place = [None] * 3
        for axis in range(3):
            place[axis] = self.pick(
                spot[self.orders[0].index(axis)], spot[self.orders[1].index(axis)]
            )
        return (place[1] * 2 + place[2], place[0] * 2 + self.core)

    def twin(self):
        return (self.gx, self.gy + 1 - 2 * self.core)

    def step(self, axis, sign):
        to = self.here[axis] + sign
        spot = tuple(to if i == axis else self.here[i] for i in range(3))
        return jnp.logical_and(to >= 0, to < self.limit[axis]), self.device(spot)


def neighbours(plan):
    flow = Flow(plan, 0)
    out = [(None, flow.twin())]
    for axis in range(3):
        for sign in (-1, 1):
            out.append(flow.step(axis, sign))
    return out


def when(condition):
    return (lambda f: f()) if condition is None else pl.when(condition)


def greet(plan, extra=()):
    barrier = pltpu.get_barrier_semaphore()
    count = jnp.int32(len(extra))
    for there, device in neighbours(plan):
        @when(there)
        def _(device=device):
            pl.semaphore_signal(barrier, inc=1, device_id=device, device_id_type=MESH)
        count = count + (1 if there is None else there.astype(jnp.int32))
    for device in extra:
        pl.semaphore_signal(barrier, inc=1, device_id=device, device_id_type=MESH)
    pl.semaphore_wait(barrier, count)


class Gather:
    def __init__(self, plan, source, target, rows, width, send_sem, recv_sem):
        self.plan, self.source, self.target, self.width = plan, source, target, width
        self.send_sem, self.recv_sem = send_sem, recv_sem
        self.cuts = [(Flow(plan, kind), *cut) for kind, cut in enumerate(rows)]

    def slot(self, cut, gx, gy):
        _, start, rows = cut
        return self.target.at[
            pl.ds(pl.multiple_of(gx * self.plan.hp + start, 16), rows),
            pl.ds(pl.multiple_of(gy * self.width, LANES), self.width),
        ]

    def copies(self, kind, cut, spot, stage, sign, own):
        flow = cut[0]
        gx, gy = flow.device(spot)
        dst = self.slot(cut, gx, gy)
        src = self.source.at[pl.ds(cut[1], cut[2]), :] if own else dst
        index = gx * (self.plan.ny // 2) + gy // 2
        goals = [(None, flow.twin(), 6)]
        for axis in range(3):
            if axis < stage:
                continue
            for direction in (-1, 1):
                there, device = flow.step(axis, direction)
                if axis == stage and not own:
                    there = jnp.logical_and(there, sign == direction)
                goals.append((there, device, 2 * axis + (direction + 1) // 2))
        out = []
        for there, device, k in goals:
            out.append((there, pltpu.make_async_remote_copy(
                src_ref=src, dst_ref=dst,
                send_sem=self.send_sem.at[kind, index, k],
                recv_sem=self.recv_sem.at[kind, gx * self.plan.ny + gy],
                device_id=device, device_id_type=MESH,
            )))
        return out

    def arrived(self, kind, cut, gx, gy):
        ref = self.slot(cut, gx, gy)
        pltpu.make_async_copy(ref, ref, self.recv_sem.at[kind, gx * self.plan.ny + gy]).wait()

    def start_own(self):
        for kind, cut in enumerate(self.cuts):
            for there, copy in self.copies(kind, cut, cut[0].here, 0, None, True):
                when(there)(copy.start)

    def walk(self, visit, phase):
        for kind, cut in enumerate(self.cuts):
            flow = cut[0]
            p, q, r = flow.here
            np_, nq, nr = flow.limit
            mp, mq, mr = flow.most

            def along_r(kk, kind=kind, cut=cut, flow=flow):
                def one(n, _):
                    k = n // mp + 1
                    op = lax.rem(n, mp)
                    for sign in (-1, 1):
                        for side in ((-1, 1) if kk else (1,)):
                            orr, oq = r - sign * k, q - side * kk
                            good = (orr >= 0) & (orr < nr) & (oq >= 0) & (oq < nq) & (op < np_)
                            pl.when(good)(functools.partial(
                                visit, kind, cut, (op, oq, orr), 2, sign))
                    return 0
                lax.fori_loop(0, (mr - 1) * mp, one, 0)

            def along_q(kk, kind=kind, cut=cut, flow=flow):
                def one(op, _):
                    for sign in (-1, 1):
                        oq = q - sign * kk
                        good = (oq >= 0) & (oq < nq) & (op < np_)
                        pl.when(good)(functools.partial(visit, kind, cut, (op, oq, r), 1, sign))
                    return 0
                lax.fori_loop(0, mp, one, 0)

            if phase == 0:
                def line(n, _, kind=kind, cut=cut):
                    k = n + 1
                    for sign in (-1, 1):
                        op = p - sign * k
                        good = (op >= 0) & (op < np_)
                        pl.when(good)(functools.partial(visit, kind, cut, (op, q, r), 0, sign))
                    return 0
                lax.fori_loop(0, mp - 1, line, 0)
            if 1 <= phase < mq:
                along_q(phase)
            if 1 <= phase <= mq:
                along_r(phase - 1)

    def phases(self):
        return max(cut[0].most[1] for cut in self.cuts) + 1

    def forward(self, phase):
        def visit(kind, cut, spot, stage, sign):
            self.arrived(kind, cut, *cut[0].device(spot))
            for there, copy in self.copies(kind, cut, spot, stage, sign, False):
                when(there)(copy.start)
        self.walk(visit, phase)

    def finish_twin(self):
        plan = self.plan
        for kind, cut in enumerate(self.cuts):
            flow = cut[0]
            def one(n, _, kind=kind, cut=cut, flow=flow):
                gx, y = n // (plan.ny // 2), lax.rem(n, plan.ny // 2)
                self.arrived(kind, cut, gx, 2 * y + 1 - flow.core)
                return 0
            lax.fori_loop(0, plan.blocks // 2, one, 0)

    def finish_sends(self):
        for kind, cut in enumerate(self.cuts):
            for there, copy in self.copies(kind, cut, cut[0].here, 0, None, True):
                when(there)(copy.wait_send)
        def visit(kind, cut, spot, stage, sign):
            for there, copy in self.copies(kind, cut, spot, stage, sign, False):
                when(there)(copy.wait_send)
        for phase in range(self.phases()):
            self.walk(visit, phase)


def gather_kernel(plan, widths, *refs):
    n = len(widths)
    sources, targets = refs[:n], refs[n:2 * n]
    send_sem, recv_sem, own_sem = refs[2 * n:]
    gx, gy = lax.axis_index("gx"), lax.axis_index("gy")
    greet(plan)
    sets = send_sem.shape[0]
    gathers = []
    for u, width in enumerate(widths):
        place = targets[u].at[
            pl.ds(pl.multiple_of(gx * plan.hp, 16), plan.hp),
            pl.ds(pl.multiple_of(gy * width, LANES), width),
        ]
        pltpu.make_async_copy(sources[u], place, own_sem.at[u]).start()
        gathers.append(Gather(plan, sources[u], targets[u], plan.cuts, width,
                              send_sem.at[u % sets], recv_sem.at[u]))
    for u, gather in enumerate(gathers):
        if u >= sets:
            gathers[u - sets].finish_sends()
        gather.start_own()
        for phase in range(gather.phases()):
            gather.forward(phase)
    for u, width in enumerate(widths):
        gathers[u].finish_twin()
        if u >= n - sets:
            gathers[u].finish_sends()
        place = targets[u].at[
            pl.ds(pl.multiple_of(gx * plan.hp, 16), plan.hp),
            pl.ds(pl.multiple_of(gy * width, LANES), width),
        ]
        pltpu.make_async_copy(sources[u], place, own_sem.at[u]).wait()


def gather_all(plan, blocks):
    widths = tuple(block.shape[1] for block in blocks)
    n = len(blocks)
    sets = n if plan.blocks <= 32 else 1
    return pl.pallas_call(
        functools.partial(gather_kernel, plan, widths),
        out_shape=[jax.ShapeDtypeStruct((plan.hh, plan.ny * w), jnp.bfloat16) for w in widths],
        in_specs=[pl.BlockSpec(memory_space=pl.ANY)] * n,
        out_specs=[pl.BlockSpec(memory_space=pl.ANY)] * n,
        scratch_shapes=[
            pltpu.SemaphoreType.DMA((sets, len(plan.cuts), plan.blocks // 2, 7)),
            pltpu.SemaphoreType.DMA((n, len(plan.cuts), plan.blocks)),
            pltpu.SemaphoreType.DMA((n,)),
        ],
        compiler_params=pltpu.CompilerParams(collective_id=0, has_side_effects=True),
    )(*blocks)


class Meet:
    def __init__(self, plan, wide, tall, send_sem, recv_sem):
        self.plan, self.wide, self.tall = plan, wide, tall
        self.send_sem, self.recv_sem = send_sem, recv_sem
        self.gx, self.gy = lax.axis_index("gx"), lax.axis_index("gy")

    @staticmethod
    def peers(plan):
        gx, gy = lax.axis_index("gx"), lax.axis_index("gy")
        return ([(lax.rem(gx + k, plan.nx), gy) for k in range(1, plan.nx)]
                + [(gx, lax.rem(gy + k, plan.ny)) for k in range(1, plan.ny)])

    def copies(self, second):
        plan = self.plan
        n = plan.ny if second else plan.nx
        ref = self.tall if second else self.wide
        own = self.gy if second else self.gx
        out = []
        for k in range(1, n):
            to = lax.rem(own + k, n)
            at = (plan.nx - 1 if second else 0) + k - 1
            out.append(pltpu.make_async_remote_copy(
                src_ref=ref.at[own], dst_ref=ref.at[own],
                send_sem=self.send_sem.at[at], recv_sem=self.recv_sem.at[at],
                device_id=(self.gx, to) if second else (to, self.gy), device_id_type=MESH,
            ))
        return out

    def run(self, value, merge, members):
        plan = self.plan
        for second in (False, True):
            ref = self.tall if second else self.wide
            ref[self.gy if second else self.gx] = value
            copies = self.copies(second)
            for copy in copies:
                copy.start()
            for copy in copies:
                copy.wait_recv()
            value = merge([ref[i] for i in range(ref.shape[0])], members)
            members = members * plan.nx
            for copy in copies:
                copy.wait_send()
        return value


def merge_sums(parts, members):
    total = parts[0]
    for part in parts[1:]:
        total = total + part
    return total


def merge_moments(parts, members):
    n = len(parts)
    mean = merge_sums([part[0:1] for part in parts], 0) / n
    squares = merge_sums([part[1:2] for part in parts], 0)
    between = merge_sums([(part[0:1] - mean) * (part[0:1] - mean) for part in parts], 0)
    return jnp.concatenate([mean, squares + members * between], axis=0)


def meet_kernel(plan, merge, x_ref, o_ref, wide, tall, send_sem, recv_sem):
    peers = Meet.peers(plan)
    barrier = pltpu.get_barrier_semaphore()
    for device in peers:
        pl.semaphore_signal(barrier, inc=1, device_id=device, device_id_type=MESH)
    pl.semaphore_wait(barrier, len(peers))
    meet = Meet(plan, wide, tall, send_sem, recv_sem)
    o_ref[...] = meet.run(x_ref[...], merge, float(plan.cells))


def meet_all(plan, value, merge, collective_id):
    rows, width = value.shape
    n = plan.nx + plan.ny - 2
    return pl.pallas_call(
        functools.partial(meet_kernel, plan, merge),
        out_shape=jax.ShapeDtypeStruct(value.shape, jnp.float32),
        in_specs=[pl.BlockSpec(memory_space=pltpu.VMEM)],
        out_specs=pl.BlockSpec(memory_space=pltpu.VMEM),
        scratch_shapes=[
            pltpu.VMEM((plan.nx, rows, width), jnp.float32),
            pltpu.VMEM((plan.ny, rows, width), jnp.float32),
            pltpu.SemaphoreType.DMA((n,)),
            pltpu.SemaphoreType.DMA((n,)),
        ],
        compiler_params=pltpu.CompilerParams(collective_id=collective_id, has_side_effects=True),
    )(value)


def share_kernel(plan, row_ref, block_ref, row_out, block_out, wide, tall, send_sem, recv_sem):
    peers = Meet.peers(plan)
    barrier = pltpu.get_barrier_semaphore()
    for device in peers:
        pl.semaphore_signal(barrier, inc=1, device_id=device, device_id_type=MESH)
    pl.semaphore_wait(barrier, len(peers))
    meet = Meet(plan, wide, tall, send_sem, recv_sem)
    wide[meet.gx] = row_ref[...]
    tall[meet.gy] = block_ref[...]
    copies = meet.copies(False) + meet.copies(True)
    for copy in copies:
        copy.start()
    for copy in copies:
        copy.wait_recv()
    row_out[...] = wide[0]
    block_out[...] = tall[0]
    for copy in copies:
        copy.wait_send()


def share_all(plan, row, block, collective_id):
    n = plan.nx + plan.ny - 2
    return pl.pallas_call(
        functools.partial(share_kernel, plan),
        out_shape=[jax.ShapeDtypeStruct(row.shape, jnp.float32),
                   jax.ShapeDtypeStruct(block.shape, jnp.float32)],
        in_specs=[pl.BlockSpec(memory_space=pltpu.VMEM)] * 2,
        out_specs=[pl.BlockSpec(memory_space=pltpu.VMEM)] * 2,
        scratch_shapes=[
            pltpu.VMEM((plan.nx, *row.shape), jnp.float32),
            pltpu.VMEM((plan.ny, *block.shape), jnp.float32),
            pltpu.SemaphoreType.DMA((n,)),
            pltpu.SemaphoreType.DMA((n,)),
        ],
        compiler_params=pltpu.CompilerParams(collective_id=collective_id, has_side_effects=True),
    )(row, block)


class Reduce:
    def __init__(self, plan, width, part, twin, slots, send_sem, twin_sem, recv_sem):
        self.plan, self.width, self.part, self.twin, self.slots = plan, width, part, twin, slots
        self.send_sem, self.twin_sem, self.recv_sem = send_sem, twin_sem, recv_sem
        self.cuts = [(Flow(plan, kind), *cut) for kind, cut in enumerate(plan.cuts)]

    @staticmethod
    def slot_counts(plan):
        counts = []
        for kind in range(len(plan.cuts)):
            sizes = (plan.ny // 2, plan.nx // 2, 2)
            first, second = (((0, 1, 2), (2, 1, 0)), ((1, 2, 0), (1, 0, 2)))[kind]
            mp, mq, mr = (max(sizes[i], sizes[j]) for i, j in zip(first, second))
            a, b, c = (Reduce.sides(m) for m in (mp, mq, mr))
            far_r = (mr > 2) * (mr * mq * mp)
            counts.append((far_r, mq * mp * (c + (mq > 2)), mp * (c + b + (mp > 2)), c + b + a))
        return counts

    @staticmethod
    def sides(most):
        return 1 if most == 2 else (2 if most > 2 else 0)

    def block(self, ref, cut, gx, gy):
        return ref.at[
            pl.ds(pl.multiple_of(gx * self.plan.hp + cut[1], 16), cut[2]),
            pl.ds(pl.multiple_of(gy * self.width, LANES), self.width),
        ]

    def twin_block(self, cut, gx, y):
        return self.twin.at[
            pl.ds(pl.multiple_of(gx * self.plan.hp + cut[1], 16), cut[2]),
            pl.ds(pl.multiple_of(y * self.width, LANES), self.width),
        ]

    def twin_copy(self, kind, cut, gx, y):
        flow = cut[0]
        return pltpu.make_async_remote_copy(
            src_ref=self.block(self.part, cut, gx, 2 * y + 1 - flow.core),
            dst_ref=self.twin_block(cut, gx, y),
            send_sem=self.twin_sem.at[0, kind, gx * (self.plan.ny // 2) + y],
            recv_sem=self.twin_sem.at[1, kind, gx * (self.plan.ny // 2) + y],
            device_id=flow.twin(), device_id_type=MESH,
        )

    def each_twin(self, visit, ys=None):
        ny2 = self.plan.ny // 2
        for kind, cut in enumerate(self.cuts):
            def one(n, _, kind=kind, cut=cut):
                visit(self.twin_copy(kind, cut, n // ny2, lax.rem(n, ny2)))
                return 0
            lax.fori_loop(0, self.plan.blocks // 2, one, 0)

    def start_twin(self):
        self.each_twin(lambda copy: copy.start())

    def entry(self, kind, stage, spot, axis, came_from):
        flow = self.cuts[kind][0]
        mp, mq, mr = flow.most
        far_r, far_q, far_p, _ = Reduce.slot_counts(self.plan)[kind]
        sides = [Reduce.sides(m) for m in flow.most]
        dp, dq, dr = spot
        if stage == 2:
            return (dr * mq + dq) * mp + dp
        if stage == 1:
            base, which = far_r, (dq * mp + dp) * (sides[2] + (mq > 2))
        elif stage == 0:
            base, which = far_r + far_q, dp * (sides[2] + sides[1] + (mp > 2))
        else:
            base, which = far_r + far_q + far_p, 0
        offset = 0
        for later in (2, 1, 0):
            if later == stage:
                return base + which + offset
            if later == axis:
                side = 0 if sides[axis] == 1 else (came_from + 1) // 2
                return base + which + offset + side
            offset += sides[later]

    def slot(self, kind, index):
        cut = self.cuts[kind]
        total = sum(Reduce.slot_counts(self.plan)[kind])
        return self.slots[kind].at[index], self.recv_sem[kind].at[index]

    def gather_terms(self, kind, cut, spot, stage, sign):
        flow = cut[0]
        ny2 = self.plan.ny // 2
        gx, gy = flow.device(spot)
        y = gy // 2
        copy = self.twin_copy(kind, cut, gx, y)
        copy.wait_recv()
        own = self.block(self.part, cut, gx, gy)
        twin = self.twin_block(cut, gx, y)
        arrivals = []
        for axis in (2, 1, 0):
            if axis > stage:
                for side in (-1, 1):
                    there, _ = flow.step(axis, side)
                    if flow.most[axis] < 2:
                        continue
                    arrivals.append((there, self.entry(kind, stage, spot, axis, side)))
            elif axis == stage and flow.most[axis] > 2:
                away = self.here_away(flow, axis, sign)
                arrivals.append((away, self.entry(kind, stage, spot, axis, None)))
        return own, twin, arrivals

    def here_away(self, flow, axis, sign):
        to = flow.here[axis] - sign
        return (to >= 0) & (to < flow.limit[axis])

    def add_in(self, kind, cut, spot, stage, sign):
        own, twin, arrivals = self.gather_terms(kind, cut, spot, stage, sign)
        own[...] = (own[...].astype(jnp.float32) + twin[...].astype(jnp.float32)).astype(jnp.bfloat16)
        for there, index in arrivals:
            slot, sem = self.slot(kind, index)
            @when(there)
            def _(slot=slot, sem=sem):
                pltpu.make_async_copy(slot, slot, sem).wait()
                own[...] = (own[...].astype(jnp.float32) + slot[...].astype(jnp.float32)).astype(
                    jnp.bfloat16)
        return own

    def onward(self, kind, cut, spot, stage, sign):
        flow = cut[0]
        _, device = self.toward(flow, stage, sign)
        gx, gy = flow.device(spot)
        to = flow.here[stage] + sign
        index_same = self.entry(kind, stage, spot, stage, None) if flow.most[stage] > 2 else None
        done = to == spot[stage]
        p_same = flow.here[0] == spot[0]
        q_same = flow.here[1] == spot[1]
        if stage == 2:
            deeper = jnp.where(q_same, jnp.where(p_same,
                               self.entry(kind, -1, spot, 2, -sign),
                               self.entry(kind, 0, spot, 2, -sign)),
                               self.entry(kind, 1, spot, 2, -sign))
        elif stage == 1:
            deeper = jnp.where(p_same, self.entry(kind, -1, spot, 1, -sign),
                               self.entry(kind, 0, spot, 1, -sign))
        else:
            deeper = self.entry(kind, -1, spot, 0, -sign)
        index = deeper if index_same is None else jnp.where(done, deeper, index_same)
        slot, sem = self.slot(kind, index)
        ny2 = self.plan.ny // 2
        return pltpu.make_async_remote_copy(
            src_ref=self.block(self.part, cut, gx, gy), dst_ref=slot,
            send_sem=self.send_sem.at[kind, gx * ny2 + gy // 2], recv_sem=sem,
            device_id=device, device_id_type=MESH,
        )

    def toward(self, flow, axis, sign):
        return flow.step(axis, sign)

    def walk(self, visit, stage):
        for kind, cut in enumerate(self.cuts):
            flow = cut[0]
            p, q, r = flow.here
            np_, nq, nr = flow.limit
            mp, mq, mr = flow.most

            def one(n, _, kind=kind, cut=cut):
                if stage == 2:
                    k, dq, dp = mr - 1 - n // (mq * mp), lax.rem(n // mp, mq), lax.rem(n, mp)
                elif stage == 1:
                    k, dp = mq - 1 - n // mp, lax.rem(n, mp)
                else:
                    k = mp - 1 - n
                for sign in (-1, 1):
                    if stage == 2:
                        d = r + sign * k
                        spot, good = (dp, dq, d), (d >= 0) & (d < nr) & (dq < nq) & (dp < np_)
                    elif stage == 1:
                        d = q + sign * k
                        spot, good = (dp, d, r), (d >= 0) & (d < nq) & (dp < np_)
                    else:
                        d = p + sign * k
                        spot, good = (d, q, r), (d >= 0) & (d < np_)
                    pl.when(good)(functools.partial(visit, kind, cut, spot, stage, sign))
                return 0
            count = {2: (mr - 1) * mq * mp, 1: (mq - 1) * mp, 0: mp - 1}[stage]
            lax.fori_loop(0, count, one, 0)

    def pass_on(self, stage):
        def visit(kind, cut, spot, stage, sign):
            self.add_in(kind, cut, spot, stage, sign)
            self.onward(kind, cut, spot, stage, sign).start()
        self.walk(visit, stage)

    def own_sum(self, out_ref, factor):
        for kind, cut in enumerate(self.cuts):
            flow = cut[0]
            own = self.add_in(kind, cut, flow.here, -1, None)
            out_ref[pl.ds(cut[1], cut[2]), :] = own[...].astype(jnp.float32) * factor

    def finish_sends(self):
        self.each_twin(lambda copy: copy.wait_send())
        def visit(kind, cut, spot, stage, sign):
            self.onward(kind, cut, spot, stage, sign).wait_send()
        for stage in (2, 1, 0):
            self.walk(visit, stage)


def reduce_kernel(plan, width, factor, x_ref, o_ref, part, twin, *rest):
    n = len(plan.cuts)
    slots, (send_sem, twin_sem), recv_sem, load_sem = rest[:n], rest[n:n + 2], rest[n + 2:2 * n + 2], rest[-1]
    load = pltpu.make_async_copy(x_ref, part, load_sem)
    load.start()
    greet(plan)
    load.wait()
    reduce = Reduce(plan, width, part, twin, slots, send_sem, twin_sem, recv_sem)
    reduce.start_twin()
    for stage in (2, 1, 0):
        reduce.pass_on(stage)
    reduce.own_sum(o_ref, factor)
    reduce.finish_sends()


def reduce_all(plan, value, factor, collective_id):
    width = value.shape[1] // plan.ny
    counts = [sum(c) for c in Reduce.slot_counts(plan)]
    return pl.pallas_call(
        functools.partial(reduce_kernel, plan, width, factor),
        out_shape=jax.ShapeDtypeStruct((plan.hp, width), jnp.float32),
        in_specs=[pl.BlockSpec(memory_space=pl.ANY)],
        out_specs=pl.BlockSpec(memory_space=pltpu.VMEM),
        scratch_shapes=[
            pltpu.VMEM((plan.hh, plan.ny * width), jnp.bfloat16),
            pltpu.VMEM((plan.hh, plan.ny // 2 * width), jnp.bfloat16),
            *[pltpu.VMEM((c, cut[1], width), jnp.bfloat16) for c, cut in zip(counts, plan.cuts)],
            pltpu.SemaphoreType.DMA((len(plan.cuts), plan.blocks // 2)),
            pltpu.SemaphoreType.DMA((2, len(plan.cuts), plan.blocks // 2)),
            *[pltpu.SemaphoreType.DMA((c,)) for c in counts],
            pltpu.SemaphoreType.DMA,
        ],
        compiler_params=pltpu.CompilerParams(
            collective_id=collective_id, has_side_effects=True, vmem_limit_bytes=60 * 1024 * 1024),
    )(value)


def rows_dot(left, right):
    return lax.dot_general(left, right, (((1,), (0,)), ((), ())), preferred_element_type=jnp.float32)


def over_cells(left, right):
    return lax.dot_general(left, right, (((1,), (1,)), ((), ())), preferred_element_type=jnp.float32)


def over_rows(left, right):
    return lax.dot_general(left, right, (((0,), (0,)), ((), ())), preferred_element_type=jnp.float32)


def pad_to(value, rows, lanes):
    return jnp.pad(value, ((0, rows - value.shape[0]), (0, lanes - value.shape[1])))


def spread_rows(plan, value):
    split = value.reshape(plan.nx, plan.h, *value.shape[1:])
    wide = jnp.pad(split, ((0, 0), (0, plan.hp - plan.h)) + ((0, 0),) * (value.ndim - 1))
    return wide.reshape(plan.hh, *value.shape[1:])


def middle_piece(plan, matrix):
    turned = matrix.T.reshape(plan.h, plan.groups, plan.h)
    wide = jnp.pad(turned, ((0, plan.hp - plan.h), (0, 0), (0, plan.hp - plan.h)))
    return pad_to(wide.reshape(plan.hp, plan.midp), plan.hp, plan.midl)


def middle_back(plan, piece):
    cut = piece[:plan.h, :plan.midp].reshape(plan.h, plan.groups, plan.hp)[:, :, :plan.h]
    return cut.reshape(plan.h, plan.mid).T


def with_row(plan, block, row, first):
    spare = jnp.where(first, row, jnp.zeros_like(row))[None]
    return pad_to(jnp.concatenate([block, spare], axis=0), plan.hp, block.shape[1])


def on_device(
    nx, ny,
    transcript_profiles,
    experiment_labels,
    measured_flags,
    retained_unit_flags,
    standard_normal_draws,
    compressor_first_matrix,
    compressor_second_matrix,
    posterior_matrix,
    posterior_intercepts,
    expander_first_matrix,
    expander_second_matrix,
    output_matrix,
    output_intercept,
    normalizer_factors,
    normalizer_translations,
):
    cells = transcript_profiles.shape[0]
    plan = Plan(nx, ny, cells, output_matrix.shape[1], output_matrix.shape[0], expander_first_matrix.shape[0])
    total_cells = float(cells * nx * ny)
    gx, gy = lax.axis_index("gx"), lax.axis_index("gy")
    first = gx == 0

    wide = jnp.concatenate([
        pad_to(compressor_first_matrix.T, plan.hp, plan.g),
        with_row(plan, output_matrix, output_intercept, first)], axis=0)
    strip = lax.ppermute(wide[:, :plan.strip], "gy", [(j + 1, j) for j in range(ny - 1)])
    wide = jnp.concatenate([wide, strip], axis=1)
    wide = pad_to(wide, 2 * plan.hp, plan.gp + plan.strip + plan.shift * ny)
    wide = lax.dynamic_slice_in_dim(wide, gy * plan.shift, plan.gp, 1)
    last = jnp.concatenate([
        expander_first_matrix.T, normalizer_factors.T, normalizer_translations.T], axis=1)
    small = jnp.concatenate([
        middle_piece(plan, compressor_second_matrix),
        middle_piece(plan, expander_second_matrix),
        pad_to(with_row(plan, posterior_matrix, posterior_intercepts, first), plan.hp, plan.ml),
        pad_to(last, plan.hp, plan.ll)], axis=1)
    embed_all, small_all, readout_all = gather_all(plan, [wide[:plan.hp], small, wide[plan.hp:]])

    parts = small_all.reshape(plan.hh, ny, plan.small)
    encoder_all = parts[:, :, plan.o2:plan.o2 + plan.midp].reshape(plan.hh, plan.hh)
    decoder_all = parts[:, :, plan.o4:plan.o4 + plan.midp].reshape(plan.hh, plan.hh)
    projector_all = parts[:, :, plan.op:plan.op + plan.moments].reshape(plan.hh, 2 * plan.latent)
    lifting_all = parts[:, 0, plan.ol:plan.ol + plan.latent]
    rows = parts[:, 0, plan.ol + plan.latent:plan.ol + plan.latent + 8].astype(jnp.float32)
    gains = [rows[:, k:k + 1] for k in range(4)]
    biases = [rows[:, 4 + k:5 + k] for k in range(4)]

    profiles = transcript_profiles.T
    draws = standard_normal_draws.T
    keepers = [
        spread_rows(plan, retained_unit_flags[k].T).astype(jnp.bfloat16) for k in range(4)]
    spare = (lax.rem(jnp.arange(plan.hh), plan.hp) == plan.h)[:, None]

    def forward_layer(hidden, k, ones, ident):
        mean = jnp.mean(hidden, axis=1)
        offset = hidden - mean[:, None]
        squares = jnp.sum(offset * offset, axis=1)
        merged = meet_all(plan, jnp.stack([mean, squares]), merge_moments, 1)
        inverse = lax.rsqrt(merged[1] / total_cells + norm_eps)[:, None]
        scaled = (hidden - merged[0][:, None]) * inverse
        normed = gains[k] * scaled + biases[k]
        keeper = keepers[k].astype(jnp.float32) * keep_scale
        active = normed * jax.nn.sigmoid(normed) * keeper
        if ones:
            active = jnp.where(spare, 1.0, active)
        return active.astype(jnp.bfloat16), normed, scaled, inverse

    def backward_layer(upstream, kept, k, loss, ident):
        _, normed, scaled, inverse = kept
        sigma = jax.nn.sigmoid(normed)
        slope = upstream * (keepers[k].astype(jnp.float32) * keep_scale) * sigma * (
            1.0 + normed * (1.0 - sigma))
        pair = jnp.stack([jnp.sum(slope, axis=1), jnp.sum(slope * scaled, axis=1),
                          jnp.full((plan.hh,), loss)])
        merged = meet_all(plan, pair, merge_sums, 2)
        shift, gain = merged[0], merged[1]
        grad = gains[k] * inverse * (
            slope - (shift[:, None] + scaled * gain[:, None]) / total_cells)
        return grad.astype(jnp.bfloat16), gain, shift, merged[2, 0]

    one = forward_layer(rows_dot(embed_all[:, :plan.genes], profiles), 0, False, 1)
    two = forward_layer(rows_dot(encoder_all, one[0]), 1, True, 2)
    moments = over_rows(projector_all, two[0])
    center, log_var = moments[:plan.latent], moments[plan.latent:]
    spread = jnp.exp(0.5 * log_var)
    sample = (center + spread * draws).astype(jnp.bfloat16)
    three = forward_layer(rows_dot(lifting_all, sample), 2, False, 3)
    four = forward_layer(rows_dot(decoder_all, three[0]), 3, True, 4)

    output = over_rows(readout_all[:, :plan.genes], four[0])
    residual = output - profiles.astype(jnp.float32)
    picker = (jnp.arange(measured_flags.shape[0], dtype=jnp.int32)[:, None]
              == experiment_labels[None, :]).astype(jnp.bfloat16)
    slab = over_rows(measured_flags.astype(jnp.bfloat16), picker)
    weighted = slab * residual
    rebuild = 0.5 * jnp.sum(weighted * residual)
    diverge = 0.5 * jnp.sum(jnp.exp(log_var) + center * center - 1.0 - log_var)
    own_loss = rebuild + kl_weight * diverge
    output_grad = weighted.astype(jnp.bfloat16)

    def frames(product):
        padded = pad_to(product, plan.hh, max(plan.frame_start) + plan.frame)
        return jnp.concatenate(
            [padded[:, s:s + plan.frame] for s in plan.frame_start], axis=1).astype(jnp.bfloat16)

    readout_part = frames(over_cells(four[0], output_grad))
    upstream = rows_dot(readout_all[:, :plan.genes], output_grad)
    grad_four, gain_four, shift_four, loss_sum = backward_layer(upstream, four, 3, own_loss, 5)
    upstream = over_rows(decoder_all, grad_four)
    grad_three, gain_three, shift_three, _ = backward_layer(upstream, three, 2, own_loss, 6)
    sample_grad = over_rows(lifting_all, grad_three)
    center_grad = sample_grad + kl_weight * center
    logvar_grad = sample_grad * 0.5 * spread * draws + kl_weight * 0.5 * (jnp.exp(log_var) - 1.0)
    moment_grad = jnp.concatenate([center_grad, logvar_grad], axis=0).astype(jnp.bfloat16)
    upstream = rows_dot(projector_all, moment_grad)
    grad_two, gain_two, shift_two, _ = backward_layer(upstream, two, 1, own_loss, 7)
    upstream = over_rows(encoder_all, grad_two)
    grad_one, gain_one, shift_one, _ = backward_layer(upstream, one, 0, own_loss, 8)
    input_grad = (over_rows(embed_all[:, :plan.genes], grad_one) - weighted).astype(jnp.bfloat16)

    encoder_part = over_cells(grad_two, one[0]).reshape(plan.hh, ny, plan.midp)
    decoder_part = over_cells(grad_four, three[0]).reshape(plan.hh, ny, plan.midp)
    projector_part = over_cells(two[0], moment_grad).reshape(plan.hh, ny, plan.moments)
    lifting_part = over_cells(grad_three, sample)

    def lanes(value, width):
        return jnp.pad(value, ((0, 0), (0, 0), (0, width - value.shape[2])))

    small_part = jnp.concatenate([
        lanes(encoder_part, plan.midl), lanes(decoder_part, plan.midl),
        lanes(projector_part, plan.ml),
        jnp.broadcast_to(pad_to(lifting_part, plan.hh, plan.ll)[:, None, :], (plan.hh, ny, plan.ll)),
    ], axis=2).reshape(plan.hh, ny * plan.small).astype(jnp.bfloat16)
    embed_part = frames(over_cells(grad_one, profiles))

    readout_sum = reduce_all(plan, readout_part, 1.0 / total_cells, 3)
    small_sum = reduce_all(plan, small_part, 1.0 / total_cells, 4)
    embed_sum = reduce_all(plan, embed_part, 1.0 / total_cells, 3)
    starts = jnp.array([plan.g * j - plan.frame_start[j] for j in range(ny)], jnp.int32)
    readout_own = lax.dynamic_slice_in_dim(readout_sum, starts[gy], plan.g, 1)
    embed_own = lax.dynamic_slice_in_dim(embed_sum, starts[gy], plan.g, 1)

    row, lifting_own = share_all(plan, jnp.concatenate([
        readout_sum[plan.h:plan.h + 1],
        small_sum[plan.h:plan.h + 1, plan.op:plan.op + plan.ml]], axis=1),
        small_sum[:, plan.ol:plan.ol + plan.ll], 5)
    baseline_own = lax.dynamic_slice_in_dim(row[0, :plan.frame], starts[gy], plan.g, 0)

    def own_units(values):
        stack = jnp.stack(values, axis=0) / total_cells
        return lax.dynamic_slice_in_dim(stack, gx * plan.hp, plan.h, 1)

    small_h = small_sum[:plan.h]
    return (
        output.astype(jnp.bfloat16).T,
        center.T,
        loss_sum / total_cells,
        input_grad.T,
        embed_own[:plan.h].T,
        middle_back(plan, small_sum[:, plan.o2:plan.o2 + plan.midl]),
        small_h[:, plan.op:plan.op + plan.moments],
        row[0, plan.frame:plan.frame + plan.moments],
        lifting_own[:plan.h, :plan.latent].T,
        middle_back(plan, small_sum[:, plan.o4:plan.o4 + plan.midl]),
        readout_own[:plan.h],
        baseline_own,
        own_units([gain_one, gain_two, gain_three, gain_four]),
        own_units([shift_one, shift_two, shift_three, shift_four]),
    )


def solution(mesh):
    return jax.shard_map(
        functools.partial(on_device, mesh.shape["gx"], mesh.shape["gy"]),
        mesh=mesh,
        in_specs=(
            P(("gx", "gy"), None),
            P(("gx", "gy")),
            P(),
            P(None, ("gx", "gy"), None),
            P(("gx", "gy"), None),
            P("gy", "gx"),
            P("gy", "gx"),
            P("gx", "gy"),
            P("gy"),
            P(None, "gx"),
            P("gy", "gx"),
            P("gx", "gy"),
            P("gy"),
            P(None, "gx"),
            P(None, "gx"),
        ),
        out_specs=(
            P(("gx", "gy"), None),
            P(("gx", "gy"), None),
            P(),
            P(("gx", "gy"), None),
            P("gy", "gx"),
            P("gy", "gx"),
            P("gx", "gy"),
            P("gy"),
            P(None, "gx"),
            P("gy", "gx"),
            P("gx", "gy"),
            P("gy"),
            P(None, "gx"),
            P(None, "gx"),
        ),
        check_vma=False,
    )
```

time: 1920 us -> 852 us (0.44)
  blocking collectives: 1210 us -> 0 us
  Pallas kernels: 0 us -> 489 us
  waiting for transfers between devices: 290 us -> 0.01 us
  local copies, waits for them, and re-layouts: 167 us -> 91.3 us
  other arithmetic: 43.1 us -> 75.5 us
    unnamed x3 -> x0, blocking collectives: 562 us -> none
    pallas_call x0 -> x13, Pallas kernels: none -> 489 us  [the longest x3 245 us: reduce_all(): pl.pallas_call(functools.partial(reduce_kernel, plan, width, factor), out...]
    psum x12 -> x0, blocking collectives: 482 us -> none  [the longest x4 165 us: normalize(): lax.psum(jnp.sum(offset * offset, axis=0), ('gx', 'gy')) / total_cells]
    all_gather x7 -> x0, blocking collectives: 168 us -> none  [the longest x1 32 us: gather_forward(): lax.all_gather(compressor_second_matrix, 'gx', axis=1, tiled=True)]
    unnamed x16 -> x0, waiting for transfers between devices: 113 us -> none
    psum x1 -> x0, waiting for transfers between devices: 95.9 us -> none  [on_device(): lax.psum((lifting_part, offsets_part, baseline_part, own_loss), ('gx', 'g...]
    unnamed x164 -> x128, local copies, waits for them, and re-layouts: 110 us -> 15.5 us
    all_gather x6 -> x0, waiting for transfers between devices: 81.9 us -> none  [the longest x1 58.9 us: gather_forward(): lax.all_gather(compressor_first_matrix, 'gx', axis=1, tiled=True)]
  transfers between devices with their start and end apart: 14 -> 1, of which waited for: 6 -> 0; matrix products, arithmetic and copies ran while one was open for 12% -> 5% of each run, Pallas kernels for 0% -> 0%
where the time goes in v1:
time: 852 us; the launch traced here: 842 us
  Pallas kernels  489 us (57%)
  matrix products  178 us (21%)
  local copies, waits for them, and re-layouts  91.3 us (11%)
  other arithmetic  75.5 us (9%)
    pallas_call x3, Pallas kernels, reduce_all(): pl.pallas_call(functools.partial(reduce_kernel, plan, width, factor), out...  245 us
    pallas_call x1, Pallas kernels, gather_all(): pl.pallas_call(functools.partial(gather_kernel, plan, widths), out_shape=...  146 us
    pallas_call x8, Pallas kernels, meet_all(): pl.pallas_call(functools.partial(meet_kernel, plan, merge), out_shape=jax...  89.4 us
    dot_general x7, matrix products, over_rows(): lax.dot_general(left, right, (((0,), (0,)), ((), ())), preferred_element_...  88.4 us
    dot_general x6, matrix products, rows_dot(): lax.dot_general(left, right, (((1,), (0,)), ((), ())), preferred_element_...  49.9 us
    dot_general x6, matrix products, over_cells(): lax.dot_general(left, right, (((1,), (1,)), ((), ())), preferred_element_...  39.7 us
  transfers between devices with their start and end apart: 1, of which 0 were waited for; matrix products, arithmetic and copies ran while one was open for 5% of the time, Pallas kernels for 0%

profile of v1, /device:TPU:26, one launch (start us, length us, event | category | flops | bytes accessed | tf_op | source)
XLA Modules:
  0.0 842.2 jit_solution(13868001490227144058)
XLA Ops:
  51.2 145.7 %shard_map.263 = (bf16[896,7168]{1,0:T(8,128)(2,1)}, bf16[896,3072]{1,0:T(8,128)(2,1)}, bf16[896,7168]{1,0:T(8,128)(2,1)}) custom-call(bf16[112,1792]{1,0:T(8,128)(2,1)} %get-tuple-element.108.refs_0_, bf16[112,768]{1,0:T(8,128)(2,1)} %fusion.40.refs_1_, bf16[112,1792]{1,0:T(8,128)(2,1)} %get-tuple-element.107.refs_2_), custom_call_target="tpu_custom_call" | custom-call | tf_op jit(solution)/shard_map/pallas_call | solution.py:272
  197.0 8.0 copy.85
  212.1 16.7 %fusion.88 = (f32[896]{0:T(1024)S(1)}, f32[896,768]{0,1:T(8,128)S(1)}) fusion(bf16[768,7000]{0,1:T(8,128)(2,1)} %param.16, bf16[896,7168]{1,0:T(8,128)(2,1)} %get-tuple-element.21), kind=kOutput, calls=%fused_computation.227 | convolution fusion | flops 9634479104 | bytes 26123776 | tf_op jit(solution)/shard_map/dot_general | solution.py:651
  230.1 12.1 %shard_map.264 = f32[2,896]{1,0:T(2,128)} custom-call(f32[2,896]{1,0:T(2,128)} %pad_maximum_fusion.7.x_ref), custom_call_target="tpu_custom_call" | custom-call | tf_op jit(solution)/shard_map/pallas_call | solution.py:359
  249.1 10.0 %shard_map.265 = f32[2,896]{1,0:T(2,128)} custom-call(f32[2,896]{1,0:T(2,128)} %pad_maximum_fusion.8.x_ref), custom_call_target="tpu_custom_call" | custom-call | tf_op jit(solution)/shard_map/pallas_call | solution.py:359
  267.3 11.8 %shard_map.266 = f32[2,896]{1,0:T(2,128)} custom-call(f32[2,896]{1,0:T(2,128)} %pad_maximum_fusion.9.x_ref), custom_call_target="tpu_custom_call" | custom-call | tf_op jit(solution)/shard_map/pallas_call | solution.py:359
  287.0 10.0 %shard_map.267 = f32[2,896]{1,0:T(2,128)} custom-call(f32[2,896]{1,0:T(2,128)} %pad_maximum_fusion.10.x_ref), custom_call_target="tpu_custom_call" | custom-call | tf_op jit(solution)/shard_map/pallas_call | solution.py:359
  302.9 20.1 %fusion.10 = f32[7000,768]{1,0:T(8,128)} fusion(bf16[896,768]{0,1:T(8,128)(2,1)S(1)} %select_convert_fusion, bf16[896,7168]{1,0:T(8,128)(2,1)} %get-tuple-element.19), kind=kOutput, calls=%fused_computation.25 | convolution fusion | flops 9633792000 | bytes 35495936 | tf_op jit(solution)/shard_map/dot_general | solution.py:659
  323.0 27.3 %multiply_reduce_fusion = (f32[]{:T(128)}, bf16[7000,768]{1,0:T(8,128)(2,1)}, bf16[768,7000]{0,1:T(8,128)(2,1)}, f32[768,7000]{0,1:T(8,128)}) fusion(f32[7000,768]{1,0:T(8,128)} %fusion.10, bf16[768,7000]{0,1:T(8,128)(2,1)} %param.16, s32[8,7000]{1,0:T(8,128)S(1)} %copy-done.25, s32[768]{0:T(1024)S(1)} %copy-done.26), kind=kOutput, calls=%fused_computation.8 | convolution fusion | flops 123710144 | bytes 75491072 | tf_op jit(solution)/shard_map/dot_general | solution.py:659
  350.4 24.9 %fusion.82 = (f32[896]{0:T(1024)S(1)}, f32[896]{0:T(1024)S(1)}, f32[896,768]{0,1:T(8,128)}) fusion(f32[896]{0:T(1024)S(1)} %get-tuple-element.81, f32[896,768]{0,1:T(8,128)} %copy-done.4, f32[896]{0:T(1024)S(1)} %get-tuple-element.80, f32[896]{0:T(1024)S(1)} %get-tuple-element.64, f32[896]{0:T(1024)S(1)} %get-tuple-element.65, f32[896,768]{0,1:T(8,128)} %copy.64, ...), kind=kOutput, calls=%fused_computation.221 | convolution fusion | flops 9644800000 | bytes 31646720 | tf_op jit(solution)/shard_map/dot_general | solution.py:651
  377.4 12.4 %shard_map.268 = f32[3,896]{1,0:T(4,128)} custom-call(f32[3,896]{1,0:T(4,128)} %maximum_maximum_fusion.x_ref), custom_call_target="tpu_custom_call" | custom-call | tf_op jit(solution)/shard_map/pallas_call | solution.py:359
  404.1 10.6 %shard_map.269 = f32[3,896]{1,0:T(4,128)} custom-call(f32[3,896]{1,0:T(4,128)} %maximum_maximum_fusion.1.x_ref), custom_call_target="tpu_custom_call" | custom-call | tf_op jit(solution)/shard_map/pallas_call | solution.py:359
  426.7 12.4 %shard_map.270 = f32[3,896]{1,0:T(4,128)} custom-call(f32[3,896]{1,0:T(4,128)} %maximum_maximum_fusion.2.x_ref), custom_call_target="tpu_custom_call" | custom-call | tf_op jit(solution)/shard_map/pallas_call | solution.py:359
  444.2 6.1 fusion.79
  464.8 6.4 fusion.18
  474.9 47.1 %shard_map.273 = f32[112,768]{1,0:T(8,128)} custom-call(bf16[896,3072]{1,0:T(8,128)(2,1)} %bitcast.150), custom_call_target="tpu_custom_call" | custom-call | tf_op jit(solution)/shard_map/pallas_call | solution.py:631
  525.9 16.1 %convolution_convert_fusion = bf16[896,7000]{1,0:T(8,128)(2,1)} fusion(bf16[896,768]{0,1:T(8,128)(2,1)} %copy-done.18, bf16[7000,768]{1,0:T(8,128)(2,1)} %get-tuple-element.89), kind=kOutput, calls=%fused_computation.18 | convolution fusion | flops 9640064000 | bytes 24672256 | tf_op jit(solution)/shard_map/dot_general | solution.py:655
  553.4 98.1 %shard_map.274 = f32[112,1920]{1,0:T(8,128)} custom-call(bf16[896,7680]{1,0:T(8,128)(2,1)} %pad_maximum_fusion.1.x_ref), custom_call_target="tpu_custom_call" | custom-call | tf_op jit(solution)/shard_map/pallas_call | solution.py:631
  652.9 8.5 %shard_map.275 = (f32[1,2048]{1,0:T(1,128)}, f32[112,128]{1,0:T(8,128)}) custom-call(f32[1,2048]{1,0:T(1,128)} %pad_maximum_fusion.6.row_ref, f32[112,128]{1,0:T(8,128)} %slice.267.block_ref), custom_call_target="tpu_custom_call" | custom-call | tf_op jit(solution)/shard_map/pallas_call | solution.py:396
  664.0 10.3 %shard_map.271 = f32[3,896]{1,0:T(4,128)} custom-call(f32[3,896]{1,0:T(4,128)} %maximum_maximum_fusion.3.x_ref), custom_call_target="tpu_custom_call" | custom-call | tf_op jit(solution)/shard_map/pallas_call | solution.py:359
  677.5 16.4 %convolution_convert_fusion.1 = bf16[896,7000]{1,0:T(8,128)(2,1)} fusion(bf16[896,768]{0,1:T(8,128)(2,1)S(1)} %multiply_convert_fusion, bf16[768,7000]{0,1:T(8,128)(2,1)} %param.16), kind=kOutput, calls=%fused_computation.19 | convolution fusion | flops 9640064000 | bytes 24672256 | tf_op jit(solution)/shard_map/dot_general | solution.py:655
  693.9 27.6 %fusion.3 = bf16[768,7000]{0,1:T(8,128)(2,1)} fusion(f32[768,7000]{0,1:T(8,128)} %get-tuple-element.130, bf16[768,7000]{0,1:T(8,128)(2,1)} %param.16, f32[7000,768]{1,0:T(8,128)} %fusion.10, bf16[896,768]{0,1:T(8,128)(2,1)} %copy-done.21, bf16[896,7168]{1,0:T(8,128)(2,1)} %get-tuple-element.21), kind=kOutput, calls=%fused_computation.5 | convolution fusion | flops 9660672000 | bytes 78503936 | tf_op jit(solution)/shard_map/dot_general | solution.py:659
  729.3 5.8 pad_maximum_fusion.x_ref
  735.1 100.0 %shard_map.272 = f32[112,1920]{1,0:T(8,128)} custom-call(bf16[896,7680]{1,0:T(8,128)(2,1)} %pad_maximum_fusion.x_ref), custom_call_target="tpu_custom_call" | custom-call | tf_op jit(solution)/shard_map/pallas_call | solution.py:631
  (258 shorter events, 170.6 us)
Async XLA Ops:
  0.6 15.0 %copy-start.27 = (bf16[200,100]{1,0:T(8,128)(2,1)S(1)}, bf16[200,100]{1,0:T(8,128)(2,1)}, u32[]{:S(2)}) copy-start(bf16[200,100]{1,0:T(8,128)(2,1)} %param.26) | copy-start | bytes 120004
  3.4 45.0 %collective-permute-start = (bf16[224,256]{1,0:T(8,128)(2,1)}, bf16[224,256]{1,0:T(8,128)(2,1)}, u32[]{:S(2)}, u32[]{:S(2)}) collective-permute-start(bf16[224,256]{1,0:T(8,128)(2,1)} %pad_maximum_fusion.5), channel_id=1, source_target_pairs={{1,0},{2,1},{3,2},{5,4},{6,5},{7,6},{9,8},{10,9},{11,10},{13,12},{... | collective-permute-start | bytes 344072 | tf_op jit(solution)/shard_map/ppermute | solution.py:715
  211.2 31.8 %copy-start.45 = (f32[896]{0:T(1024)}, f32[896]{0:T(1024)S(1)}, u32[]{:S(2)}) copy-start(f32[896]{0:T(1024)S(1)} %get-tuple-element.69) | copy-start | bytes 10756
  211.2 31.8 %copy-start.47 = (f32[896]{0:T(1024)}, f32[896]{0:T(1024)S(1)}, u32[]{:S(2)}) copy-start(f32[896]{0:T(1024)S(1)} %get-tuple-element.70) | copy-start | bytes 10756
  211.2 48.6 %copy-start.49 = (f32[896]{0:T(1024)}, f32[896]{0:T(1024)S(1)}, u32[]{:S(2)}) copy-start(f32[896]{0:T(1024)S(1)} %get-tuple-element.68) | copy-start | bytes 10756
  211.2 48.6 %copy-start.51 = (f32[896]{0:T(1024)}, f32[896]{0:T(1024)S(1)}, u32[]{:S(2)}) copy-start(f32[896]{0:T(1024)S(1)} %get-tuple-element.71) | copy-start | bytes 10756
  228.8 17.1 %copy-start = (f32[896,768]{0,1:T(8,128)}, f32[896,768]{0,1:T(8,128)S(1)}, u32[]{:S(2)}) copy-start(f32[896,768]{0,1:T(8,128)S(1)} %get-tuple-element.123) | copy-start | bytes 8257540
  247.8 15.6 %copy-start.2 = (f32[896,768]{0,1:T(8,128)}, f32[896,768]{0,1:T(8,128)S(1)}, u32[]{:S(2)}) copy-start(f32[896,768]{0,1:T(8,128)S(1)} %get-tuple-element.125) | copy-start | bytes 8257540
  247.8 12.7 %copy-start.59 = (pred[896]{0:T(1024)(128)(4,1)S(1)}, pred[896]{0:T(1024)(128)(4,1)}, u32[]{:S(2)}) copy-start(pred[896]{0:T(1024)(128)(4,1)} %remainder_compare_fusion) | copy-start | bytes 2692
  302.9 20.1 %copy-start.18 = (bf16[896,768]{0,1:T(8,128)(2,1)}, bf16[896,768]{0,1:T(8,128)(2,1)S(1)}, u32[]{:S(2)}) copy-start(bf16[896,768]{0,1:T(8,128)(2,1)S(1)} %select_convert_fusion) | copy-start | bytes 4128772
  302.9 20.1 %copy-start.25 = (s32[8,7000]{1,0:T(8,128)S(1)}, s32[8,7000]{1,0:T(8,128)}, u32[]{:S(2)}) copy-start(s32[8,7000]{1,0:T(8,128)} %param.18) | copy-start | bytes 672004
  302.9 20.1 %copy-start.26 = (s32[768]{0:T(1024)S(1)}, s32[768]{0:T(1024)}, u32[]{:S(2)}) copy-start(s32[768]{0:T(1024)} %param.17) | copy-start | bytes 9220
  350.4 42.0 %copy-start.44 = (f32[896]{0:T(1024)S(1)}, f32[896]{0:T(1024)}, u32[]{:S(2)}) copy-start(f32[896]{0:T(1024)} %get-tuple-element.61) | copy-start | bytes 10756
  400.6 15.5 %copy-start.43 = (f32[896]{0:T(1024)S(1)}, f32[896]{0:T(1024)}, u32[]{:S(2)}) copy-start(f32[896]{0:T(1024)} %get-tuple-element.62) | copy-start | bytes 10756
  416.1 6.1 copy-start.9
  422.7 17.2 %copy-start.42 = (f32[896]{0:T(1024)S(1)}, f32[896]{0:T(1024)}, u32[]{:S(2)}) copy-start(f32[896]{0:T(1024)} %get-tuple-element.63) | copy-start | bytes 10756
  444.2 6.1 copy-start.17
  459.0 5.5 copy-start.24
  553.4 121.7 %copy-start.41 = (f32[896]{0:T(1024)S(1)}, f32[896]{0:T(1024)}, u32[]{:S(2)}) copy-start(f32[896]{0:T(1024)} %get-tuple-element.60) | copy-start | bytes 10756
  677.5 16.4 %copy-start.21 = (bf16[896,768]{0,1:T(8,128)(2,1)}, bf16[896,768]{0,1:T(8,128)(2,1)S(1)}, u32[]{:S(2)}) copy-start(bf16[896,768]{0,1:T(8,128)(2,1)S(1)} %multiply_convert_fusion) | copy-start | bytes 4128772
  735.1 100.0 %copy-start.28 = (f32[112,128]{1,0:T(8,128)S(1)}, f32[112,128]{1,0:T(8,128)}, u32[]{:S(2)}) copy-start(f32[112,128]{1,0:T(8,128)} %get-tuple-element.23) | copy-start | bytes 172036
  735.1 100.8 %copy-start.10 = (f32[112,1920]{1,0:T(8,128)S(1)}, f32[112,1920]{1,0:T(8,128)}, u32[]{:S(2)}) copy-start(f32[112,1920]{1,0:T(8,128)} %shard_map.274) | copy-start | bytes 2580484
  835.0 4.8 copy-start.55
  835.1 4.8 copy-start.56
  (37 other events, 125.2 us)

commit v2 on v1

--- a/solution.py
+++ b/solution.py
@@ -112,10 +112,11 @@
 
 
 class Gather:
-    def __init__(self, plan, source, target, rows, width, send_sem, recv_sem):
+    def __init__(self, plan, source, target, width, send_sem, recv_sem):
         self.plan, self.source, self.target, self.width = plan, source, target, width
         self.send_sem, self.recv_sem = send_sem, recv_sem
-        self.cuts = [(Flow(plan, kind), *cut) for kind, cut in enumerate(rows)]
+        self.cuts = [(Flow(plan, kind), *cut) for kind, cut in enumerate(plan.cuts)]
+        self.phases = 1 + max(sum(m - 1 for m in cut[0].most) for cut in self.cuts)
 
     def slot(self, cut, gx, gy):
         _, start, rows = cut
@@ -124,21 +125,35 @@
             pl.ds(pl.multiple_of(gy * self.width, LANES), self.width),
         ]
 
-    def copies(self, kind, cut, spot, stage, sign, own):
+    def own_copy(self, sem):
+        plan = self.plan
+        gx, gy = lax.axis_index("gx"), lax.axis_index("gy")
+        place = self.target.at[
+            pl.ds(pl.multiple_of(gx * plan.hp, 16), plan.hp),
+            pl.ds(pl.multiple_of(gy * self.width, LANES), self.width),
+        ]
+        return pltpu.make_async_copy(self.source, place, sem)
+
+    def copies(self, kind, cut, spot, own):
         flow = cut[0]
         gx, gy = flow.device(spot)
         dst = self.slot(cut, gx, gy)
         src = self.source.at[pl.ds(cut[1], cut[2]), :] if own else dst
         index = gx * (self.plan.ny // 2) + gy // 2
         goals = [(None, flow.twin(), 6)]
-        for axis in range(3):
-            if axis < stage:
-                continue
-            for direction in (-1, 1):
-                there, device = flow.step(axis, direction)
-                if axis == stage and not own:
-                    there = jnp.logical_and(there, sign == direction)
-                goals.append((there, device, 2 * axis + (direction + 1) // 2))
+        level = None
+        for axis in (2, 1, 0):
+            for sign in (-1, 1):
+                if flow.most[axis] < 2:
+                    continue
+                there, device = flow.step(axis, sign)
+                if not own:
+                    there = there & ((flow.here[axis] - spot[axis]) * sign >= 0)
+                    if level is not None:
+                        there = there & level
+                goals.append((there, device, 2 * axis + (sign + 1) // 2))
+            same = spot[axis] == flow.here[axis]
+            level = same if level is None else level & same
         out = []
         for there, device, k in goals:
             out.append((there, pltpu.make_async_remote_copy(
@@ -155,61 +170,32 @@
 
     def start_own(self):
         for kind, cut in enumerate(self.cuts):
-            for there, copy in self.copies(kind, cut, cut[0].here, 0, None, True):
+            for there, copy in self.copies(kind, cut, cut[0].here, True):
                 when(there)(copy.start)
 
-    def walk(self, visit, phase):
+    def walk(self, visit, phase=None):
         for kind, cut in enumerate(self.cuts):
             flow = cut[0]
-            p, q, r = flow.here
-            np_, nq, nr = flow.limit
             mp, mq, mr = flow.most
 
-            def along_r(kk, kind=kind, cut=cut, flow=flow):
-                def one(n, _):
-                    k = n // mp + 1
-                    op = lax.rem(n, mp)
-                    for sign in (-1, 1):
-                        for side in ((-1, 1) if kk else (1,)):
-                            orr, oq = r - sign * k, q - side * kk
-                            good = (orr >= 0) & (orr < nr) & (oq >= 0) & (oq < nq) & (op < np_)
-                            pl.when(good)(functools.partial(
-                                visit, kind, cut, (op, oq, orr), 2, sign))
-                    return 0
-                lax.fori_loop(0, (mr - 1) * mp, one, 0)
-
-            def along_q(kk, kind=kind, cut=cut, flow=flow):
-                def one(op, _):
-                    for sign in (-1, 1):
-                        oq = q - sign * kk
-                        good = (oq >= 0) & (oq < nq) & (op < np_)
-                        pl.when(good)(functools.partial(visit, kind, cut, (op, oq, r), 1, sign))
-                    return 0
-                lax.fori_loop(0, mp, one, 0)
-
-            if phase == 0:
-                def line(n, _, kind=kind, cut=cut):
-                    k = n + 1
-                    for sign in (-1, 1):
-                        op = p - sign * k
-                        good = (op >= 0) & (op < np_)
-                        pl.when(good)(functools.partial(visit, kind, cut, (op, q, r), 0, sign))
-                    return 0
-                lax.fori_loop(0, mp - 1, line, 0)
-            if 1 <= phase < mq:
-                along_q(phase)
-            if 1 <= phase <= mq:
-                along_r(phase - 1)
-
-    def phases(self):
-        return max(cut[0].most[1] for cut in self.cuts) + 1
+            def one(n, _, kind=kind, cut=cut, flow=flow):
+                spot = (lax.rem(n, mp), lax.rem(n // mp, mq), n // (mp * mq))
+                hops, good = 0, None
+                for here, limit, at in zip(flow.here, flow.limit, spot):
+                    hops = hops + jnp.abs(at - here)
+                    good = at < limit if good is None else good & (at < limit)
+                good = good & ((hops > 0) if phase is None else (hops == phase))
+                pl.when(good)(functools.partial(visit, kind, cut, spot))
+                return 0
+            lax.fori_loop(0, mp * mq * mr, one, 0)
 
     def forward(self, phase):
-        def visit(kind, cut, spot, stage, sign):
+        def visit(kind, cut, spot):
             self.arrived(kind, cut, *cut[0].device(spot))
-            for there, copy in self.copies(kind, cut, spot, stage, sign, False):
+            for there, copy in self.copies(kind, cut, spot, False):
                 when(there)(copy.start)
-        self.walk(visit, phase)
+        if phase < self.phases:
+            self.walk(visit, phase)
 
     def finish_twin(self):
         plan = self.plan
@@ -223,64 +209,12 @@
 
     def finish_sends(self):
         for kind, cut in enumerate(self.cuts):
-            for there, copy in self.copies(kind, cut, cut[0].here, 0, None, True):
+            for there, copy in self.copies(kind, cut, cut[0].here, True):
                 when(there)(copy.wait_send)
-        def visit(kind, cut, spot, stage, sign):
-            for there, copy in self.copies(kind, cut, spot, stage, sign, False):
+        def visit(kind, cut, spot):
+            for there, copy in self.copies(kind, cut, spot, False):
                 when(there)(copy.wait_send)
-        for phase in range(self.phases()):
-            self.walk(visit, phase)
-
-
-def gather_kernel(plan, widths, *refs):
-    n = len(widths)
-    sources, targets = refs[:n], refs[n:2 * n]
-    send_sem, recv_sem, own_sem = refs[2 * n:]
-    gx, gy = lax.axis_index("gx"), lax.axis_index("gy")
-    greet(plan)
-    sets = send_sem.shape[0]
-    gathers = []
-    for u, width in enumerate(widths):
-        place = targets[u].at[
-            pl.ds(pl.multiple_of(gx * plan.hp, 16), plan.hp),
-            pl.ds(pl.multiple_of(gy * width, LANES), width),
-        ]
-        pltpu.make_async_copy(sources[u], place, own_sem.at[u]).start()
-        gathers.append(Gather(plan, sources[u], targets[u], plan.cuts, width,
-                              send_sem.at[u % sets], recv_sem.at[u]))
-    for u, gather in enumerate(gathers):
-        if u >= sets:
-            gathers[u - sets].finish_sends()
-        gather.start_own()
-        for phase in range(gather.phases()):
-            gather.forward(phase)
-    for u, width in enumerate(widths):
-        gathers[u].finish_twin()
-        if u >= n - sets:
-            gathers[u].finish_sends()
-        place = targets[u].at[
-            pl.ds(pl.multiple_of(gx * plan.hp, 16), plan.hp),
-            pl.ds(pl.multiple_of(gy * width, LANES), width),
-        ]
-        pltpu.make_async_copy(sources[u], place, own_sem.at[u]).wait()
-
-
-def gather_all(plan, blocks):
-    widths = tuple(block.shape[1] for block in blocks)
-    n = len(blocks)
-    sets = n if plan.blocks <= 32 else 1
-    return pl.pallas_call(
-        functools.partial(gather_kernel, plan, widths),
-        out_shape=[jax.ShapeDtypeStruct((plan.hh, plan.ny * w), jnp.bfloat16) for w in widths],
-        in_specs=[pl.BlockSpec(memory_space=pl.ANY)] * n,
-        out_specs=[pl.BlockSpec(memory_space=pl.ANY)] * n,
-        scratch_shapes=[
-            pltpu.SemaphoreType.DMA((sets, len(plan.cuts), plan.blocks // 2, 7)),
-            pltpu.SemaphoreType.DMA((n, len(plan.cuts), plan.blocks)),
-            pltpu.SemaphoreType.DMA((n,)),
-        ],
-        compiler_params=pltpu.CompilerParams(collective_id=0, has_side_effects=True),
-    )(*blocks)
+        self.walk(visit)
 
 
 class Meet:
@@ -311,7 +245,7 @@
             ))
         return out
 
-    def run(self, value, merge, members):
+    def run(self, value, merge, members, between=None):
         plan = self.plan
         for second in (False, True):
             ref = self.tall if second else self.wide
@@ -319,6 +253,8 @@
             copies = self.copies(second)
             for copy in copies:
                 copy.start()
+            if between is not None:
+                between(second)
             for copy in copies:
                 copy.wait_recv()
             value = merge([ref[i] for i in range(ref.shape[0])], members)
@@ -341,6 +277,279 @@
     squares = merge_sums([part[1:2] for part in parts], 0)
     between = merge_sums([(part[0:1] - mean) * (part[0:1] - mean) for part in parts], 0)
     return jnp.concatenate([mean, squares + members * between], axis=0)
+
+
+def tiled(column, plan):
+    return jnp.concatenate([column] * (plan.cells // LANES), axis=1)
+
+
+def lane_sums(value):
+    total = value[:, :LANES]
+    for at in range(LANES, value.shape[1], LANES):
+        total = total + value[:, at:at + LANES]
+    return total
+
+
+def as_row(value):
+    return jnp.sum(value.T, axis=0, keepdims=True)
+
+
+def as_column(row):
+    return jnp.broadcast_to(row, (LANES, LANES)).T
+
+
+def aligned(start, rows=LANES):
+    return pl.ds(pl.multiple_of(start, rows), rows)
+
+
+def moment_rows(plan, h_ref, row_ref):
+    def block(i, _):
+        value = h_ref[aligned(i * LANES), :]
+        sums = lane_sums(value)
+        mean = jnp.sum(sums, axis=1, keepdims=True) / plan.cells
+        offset = value - mean
+        row_ref[0:1, aligned(i * LANES)] = as_row(sums) / plan.cells
+        row_ref[1:2, aligned(i * LANES)] = as_row(lane_sums(offset * offset))
+        return 0
+    lax.fori_loop(0, plan.hh // LANES, block, 0)
+
+
+def unit_column(plan, small_ref, i, lane):
+    slab = small_ref[aligned(i * LANES), plan.ol + plan.ll - LANES:plan.ol + plan.ll]
+    at = lane - (plan.ll - LANES)
+    return jnp.broadcast_to(slab.astype(jnp.float32)[:, at:at + 1], (LANES, LANES))
+
+
+def activate(plan, k, h_ref, row_ref, small_ref, keep_ref, out_ref, column_ref, total_cells, spare):
+    def block(i, _):
+        column_ref[0] = as_column(row_ref[0:1, aligned(i * LANES)])
+        column_ref[1] = as_column(lax.rsqrt(row_ref[1:2, aligned(i * LANES)] / total_cells + norm_eps))
+        column_ref[2] = unit_column(plan, small_ref, i, plan.latent + k)
+        column_ref[3] = unit_column(plan, small_ref, i, plan.latent + 4 + k)
+
+        def chunk(j, _):
+            rows = aligned(i * LANES + j * 16, 16)
+            mean, inverse, gain, bias = (
+                tiled(column_ref[n, aligned(j * 16, 16), :], plan) for n in range(4))
+            scaled = (h_ref[rows, :] - mean) * inverse
+            h_ref[rows, :] = scaled
+            normed = gain * scaled + bias
+            active = normed * jax.nn.sigmoid(normed) * keep_ref[k, rows, :].astype(jnp.float32)
+            if spare:
+                row = lax.broadcasted_iota(jnp.int32, active.shape, 0) + (i * LANES + j * 16)
+                active = jnp.where(lax.rem(row, plan.hp) == plan.h, 1.0, active)
+            out_ref[rows, :] = active.astype(jnp.bfloat16)
+            return 0
+        lax.fori_loop(0, LANES // 16, chunk, 0)
+        return 0
+    lax.fori_loop(0, plan.hh // LANES, block, 0)
+
+
+def keep_rows(plan, flags_ref, keep_ref, k):
+    def lane(t, _):
+        lanes = aligned(t * LANES)
+        for group in range(plan.nx):
+            for start in range(0, plan.hp, 16):
+                at = group * plan.h + start
+                value = flags_ref[at:at + 16, lanes].astype(jnp.float32) * keep_scale
+                if start + 16 > plan.h:
+                    row = lax.broadcasted_iota(jnp.int32, value.shape, 0)
+                    value = jnp.where(row < plan.h - start, value, 0.0)
+                at = group * plan.hp + start
+                keep_ref[k, at:at + 16, lanes] = value.astype(jnp.bfloat16)
+        return 0
+    lax.fori_loop(0, plan.cells // LANES, lane, 0)
+
+
+def forward_kernel(plan, total_cells, *refs):
+    (w1, wsmall, wout, x_hbm, flags_hbm, draws_ref,
+     embed_all, small_out, readout_all, center_out, log_var_out, sample_out, layers_out, scaled_out,
+     keep_out, rows_out,
+     w1_ref, small_ref, x_ref, keep_ref, flags_ref, h_ref, layer_ref, column_ref, latent_ref,
+     wide, tall, send_sem, recv_sem, meet_send, meet_recv, own_sem, load_sem, flag_sem, out_sem) = refs
+    mid = plan.midp
+    load = pltpu.make_async_copy(x_hbm, x_ref, load_sem)
+    deep = flags_ref.shape[0]
+
+    def flags(k):
+        return pltpu.make_async_copy(
+            flags_hbm.at[k], flags_ref.at[k % deep, pl.ds(0, plan.hidden), :], flag_sem.at[k % deep])
+
+    for k in range(deep):
+        flags(k).start()
+    load.start()
+    sets = send_sem.shape[0]
+    embed, small, readout = (
+        Gather(plan, source, target, width, send_sem.at[u % sets], recv_sem.at[u])
+        for u, (source, target, width) in enumerate((
+            (w1, w1_ref, plan.gp), (wsmall, small_ref, plan.small), (wout, readout_all, plan.gp))))
+    own = [g.own_copy(own_sem.at[u]) for u, g in enumerate((embed, small, readout))]
+    for copy in own:
+        copy.start()
+    peers = Meet.peers(plan)
+    barrier = pltpu.get_barrier_semaphore()
+    for device in peers:
+        pl.semaphore_signal(barrier, inc=1, device_id=device, device_id_type=MESH)
+    pl.semaphore_wait(barrier, len(peers))
+
+    def keepers(k):
+        flags(k).wait()
+        keep_rows(plan, flags_ref.at[k % deep], keep_ref, k)
+        if k + deep < 4:
+            flags(k + deep).start()
+
+    embed.start_own()
+    late = embed.phases - 2
+    for phase in range(1, embed.phases):
+        if phase <= 4:
+            keepers(phase - 1)
+        if phase == late:
+            if sets == 1:
+                pass
+            else:
+                small.start_own()
+        embed.forward(phase)
+    for k in range(embed.phases - 1, 4):
+        keepers(k)
+    if sets == 1:
+        embed.finish_sends()
+        small.start_own()
+    load.wait()
+    tail = layer_ref.shape[1] - plan.hh
+    for k in range(4):
+        if tail:
+            layer_ref[k, plan.hh:, :] = jnp.zeros((tail, plan.cells), jnp.bfloat16)
+    latent_ref[...] = jnp.zeros_like(latent_ref)
+    latent_ref[2, 0:plan.latent, :] = draws_ref[...]
+    own[0].wait()
+    embed.finish_twin()
+    outs = [pltpu.make_async_copy(w1_ref, embed_all, out_sem.at[0])]
+    outs[0].start()
+
+    done = 1
+    for j in range(plan.ny):
+        start, stop = j * plan.gp, min((j + 1) * plan.gp, plan.genes)
+        part = rows_dot(w1_ref[:, start:stop], x_ref[start:stop, :])
+        h_ref[0] = part if j == 0 else h_ref[0] + part
+        if done < small.phases:
+            small.forward(done)
+            done += 1
+        if j == 1 and sets > 1:
+            readout.start_own()
+    while done < small.phases:
+        small.forward(done)
+        done += 1
+    own[1].wait()
+    small.finish_twin()
+    if sets == 1:
+        small.finish_sends()
+        readout.start_own()
+    outs.append(pltpu.make_async_copy(small_ref, small_out, out_sem.at[1]))
+    outs[-1].start()
+    own[2].wait()
+
+    state = {"phase": 1}
+
+    def between(second):
+        if state["phase"] < readout.phases:
+            readout.forward(state["phase"])
+            state["phase"] += 1
+
+    def norm(k, spare):
+        h = h_ref.at[k % 2]
+        moment_rows(plan, h, rows_out.at[k])
+        meet = Meet(plan, wide.at[k], tall.at[k], meet_send.at[k], meet_recv.at[k])
+        rows_out[k] = meet.run(rows_out[k], merge_moments, float(plan.cells), between)
+        activate(plan, k, h, rows_out.at[k], small_ref, keep_ref, layer_ref.at[k], column_ref,
+                 total_cells, spare)
+        for n, (source, target) in enumerate((
+                (h, scaled_out.at[k]),
+                (layer_ref.at[k, pl.ds(0, plan.hh), :], layers_out.at[k]),
+                (keep_ref.at[k], keep_out.at[k]))):
+            outs.append(pltpu.make_async_copy(source, target, out_sem.at[3 + 3 * k + n]))
+            outs[-1].start()
+        return outs[-3]
+
+    def hidden(source, lane, target):
+        for j in range(plan.ny):
+            at = j * plan.small + lane
+            part = rows_dot(small_ref[:, at:at + plan.midl], source[mid * j:mid * j + plan.midl, :])
+            target[...] = part if j == 0 else target[...] + part
+
+    wrote_one = norm(0, False)
+    hidden(layer_ref.at[0], plan.o2, h_ref.at[1])
+    wrote_two = norm(1, True)
+    half = plan.ny // 2
+    for j in range(plan.ny):
+        at = j * plan.small + plan.op
+        part = over_rows(small_ref[:, at:at + plan.ml], layer_ref[1, 0:plan.hh, :])
+        spot = (j % half) * plan.moments
+        latent_ref[j // half, spot:spot + plan.moments, :] = part[:plan.moments]
+    center, log_var = latent_ref[0], latent_ref[1]
+    sample = center + jnp.exp(0.5 * log_var) * latent_ref[2]
+    row = lax.broadcasted_iota(jnp.int32, sample.shape, 0)
+    sample_out[...] = jnp.where(row < plan.latent, sample, 0.0).astype(jnp.bfloat16)
+    center_out[...] = latent_ref[0, 0:plan.latent, :]
+    log_var_out[...] = latent_ref[1, 0:plan.latent, :]
+    wrote_one.wait()
+    h_ref[0] = rows_dot(small_ref[:, plan.ol:plan.ol + plan.ll], sample_out[...])
+    norm(2, False)
+    wrote_two.wait()
+    hidden(layer_ref.at[2], plan.o4, h_ref.at[1])
+    norm(3, True)
+    while state["phase"] < readout.phases:
+        between(False)
+    readout.finish_twin()
+    if sets > 1:
+        embed.finish_sends()
+        small.finish_sends()
+    readout.finish_sends()
+    for copy in outs:
+        if copy is not wrote_one and copy is not wrote_two:
+            copy.wait()
+
+
+def forward_all(plan, total_cells, w1, wsmall, wout, profiles, flags, draws):
+    any_spec, vmem = pl.BlockSpec(memory_space=pl.ANY), pl.BlockSpec(memory_space=pltpu.VMEM)
+    f32, bf16 = jnp.float32, jnp.bfloat16
+    n = plan.nx + plan.ny - 2
+    cuts = len(plan.cuts)
+    sets = 3 if plan.blocks <= 32 else 1
+    shape = jax.ShapeDtypeStruct
+    return pl.pallas_call(
+        functools.partial(forward_kernel, plan, total_cells),
+        out_shape=[
+            shape((plan.hh, plan.gg), bf16), shape((plan.hh, plan.ny * plan.small), bf16),
+            shape((plan.hh, plan.gg), bf16), shape((plan.latent, plan.cells), f32),
+            shape((plan.latent, plan.cells), f32), shape((plan.ll, plan.cells), bf16),
+            shape((4, plan.hh, plan.cells), bf16), shape((4, plan.hh, plan.cells), f32),
+            shape((4, plan.hh, plan.cells), bf16), shape((4, 2, plan.hh), f32)],
+        in_specs=[any_spec] * 5 + [vmem],
+        out_specs=[any_spec] * 3 + [vmem] * 3 + [any_spec] * 3 + [vmem],
+        scratch_shapes=[
+            pltpu.VMEM((plan.hh, plan.gg), bf16),
+            pltpu.VMEM((plan.hh, plan.ny * plan.small), bf16),
+            pltpu.VMEM((plan.genes, plan.cells), bf16),
+            pltpu.VMEM((4, plan.hh, plan.cells), bf16),
+            pltpu.VMEM((2 if sets > 1 else 1, plan.hidden + 16, plan.cells), jnp.int32),
+            pltpu.VMEM((2, plan.hh, plan.cells), f32),
+            pltpu.VMEM((4, plan.hh + plan.midl - plan.midp, plan.cells), bf16),
+            pltpu.VMEM((4, LANES, LANES), f32),
+            pltpu.VMEM((3, plan.ll, plan.cells), f32),
+            pltpu.VMEM((4, plan.nx, 2, plan.hh), f32),
+            pltpu.VMEM((4, plan.ny, 2, plan.hh), f32),
+            pltpu.SemaphoreType.DMA((sets, cuts, plan.blocks // 2, 7)),
+            pltpu.SemaphoreType.DMA((3, cuts, plan.blocks)),
+            pltpu.SemaphoreType.DMA((4, n)),
+            pltpu.SemaphoreType.DMA((4, n)),
+            pltpu.SemaphoreType.DMA((3,)),
+            pltpu.SemaphoreType.DMA,
+            pltpu.SemaphoreType.DMA((2,)),
+            pltpu.SemaphoreType.DMA((15,)),
+        ],
+        compiler_params=pltpu.CompilerParams(
+            collective_id=0, has_side_effects=True, vmem_limit_bytes=60 * 1024 * 1024),
+    )(w1, wsmall, wout, profiles, flags, draws)
 
 
 def meet_kernel(plan, merge, x_ref, o_ref, wide, tall, send_sem, recv_sem):
@@ -663,12 +872,6 @@
     return jnp.pad(value, ((0, rows - value.shape[0]), (0, lanes - value.shape[1])))
 
 
-def spread_rows(plan, value):
-    split = value.reshape(plan.nx, plan.h, *value.shape[1:])
-    wide = jnp.pad(split, ((0, 0), (0, plan.hp - plan.h)) + ((0, 0),) * (value.ndim - 1))
-    return wide.reshape(plan.hh, *value.shape[1:])
-
-
 def middle_piece(plan, matrix):
     turned = matrix.T.reshape(plan.h, plan.groups, plan.h)
     wide = jnp.pad(turned, ((0, plan.hp - plan.h), (0, 0), (0, plan.hp - plan.h)))
@@ -723,8 +926,12 @@
         middle_piece(plan, expander_second_matrix),
         pad_to(with_row(plan, posterior_matrix, posterior_intercepts, first), plan.hp, plan.ml),
         pad_to(last, plan.hp, plan.ll)], axis=1)
-    embed_all, small_all, readout_all = gather_all(plan, [wide[:plan.hp], small, wide[plan.hp:]])
-
+    profiles = transcript_profiles.T
+    draws = standard_normal_draws.T
+    (embed_all, small_all, readout_all, center, log_var, sample, layers, scaled_values, keep_values,
+     norm_rows) = forward_all(
+        plan, total_cells, wide[:plan.hp], small, wide[plan.hp:], profiles,
+        jnp.swapaxes(retained_unit_flags, 1, 2), draws)
     parts = small_all.reshape(plan.hh, ny, plan.small)
     encoder_all = parts[:, :, plan.o2:plan.o2 + plan.midp].reshape(plan.hh, plan.hh)
     decoder_all = parts[:, :, plan.o4:plan.o4 + plan.midp].reshape(plan.hh, plan.hh)
@@ -734,30 +941,18 @@
     gains = [rows[:, k:k + 1] for k in range(4)]
     biases = [rows[:, 4 + k:5 + k] for k in range(4)]
 
-    profiles = transcript_profiles.T
-    draws = standard_normal_draws.T
-    keepers = [
-        spread_rows(plan, retained_unit_flags[k].T).astype(jnp.bfloat16) for k in range(4)]
-    spare = (lax.rem(jnp.arange(plan.hh), plan.hp) == plan.h)[:, None]
-
-    def forward_layer(hidden, k, ones, ident):
-        mean = jnp.mean(hidden, axis=1)
-        offset = hidden - mean[:, None]
-        squares = jnp.sum(offset * offset, axis=1)
-        merged = meet_all(plan, jnp.stack([mean, squares]), merge_moments, 1)
-        inverse = lax.rsqrt(merged[1] / total_cells + norm_eps)[:, None]
-        scaled = (hidden - merged[0][:, None]) * inverse
-        normed = gains[k] * scaled + biases[k]
-        keeper = keepers[k].astype(jnp.float32) * keep_scale
-        active = normed * jax.nn.sigmoid(normed) * keeper
-        if ones:
-            active = jnp.where(spare, 1.0, active)
-        return active.astype(jnp.bfloat16), normed, scaled, inverse
+    spread = jnp.exp(0.5 * log_var)
+
+    def kept_layer(k):
+        inverse = lax.rsqrt(norm_rows[k, 1] / total_cells + norm_eps)[:, None]
+        return layers[k], gains[k] * scaled_values[k] + biases[k], scaled_values[k], inverse
+
+    one, two, three, four = (kept_layer(k) for k in range(4))
 
     def backward_layer(upstream, kept, k, loss, ident):
         _, normed, scaled, inverse = kept
         sigma = jax.nn.sigmoid(normed)
-        slope = upstream * (keepers[k].astype(jnp.float32) * keep_scale) * sigma * (
+        slope = upstream * keep_values[k].astype(jnp.float32) * sigma * (
             1.0 + normed * (1.0 - sigma))
         pair = jnp.stack([jnp.sum(slope, axis=1), jnp.sum(slope * scaled, axis=1),
                           jnp.full((plan.hh,), loss)])
@@ -766,15 +961,6 @@
         grad = gains[k] * inverse * (
             slope - (shift[:, None] + scaled * gain[:, None]) / total_cells)
         return grad.astype(jnp.bfloat16), gain, shift, merged[2, 0]
-
-    one = forward_layer(rows_dot(embed_all[:, :plan.genes], profiles), 0, False, 1)
-    two = forward_layer(rows_dot(encoder_all, one[0]), 1, True, 2)
-    moments = over_rows(projector_all, two[0])
-    center, log_var = moments[:plan.latent], moments[plan.latent:]
-    spread = jnp.exp(0.5 * log_var)
-    sample = (center + spread * draws).astype(jnp.bfloat16)
-    three = forward_layer(rows_dot(lifting_all, sample), 2, False, 3)
-    four = forward_layer(rows_dot(decoder_all, three[0]), 3, True, 4)
 
     output = over_rows(readout_all[:, :plan.genes], four[0])
     residual = output - profiles.astype(jnp.float32)
@@ -797,7 +983,7 @@
     grad_four, gain_four, shift_four, loss_sum = backward_layer(upstream, four, 3, own_loss, 5)
     upstream = over_rows(decoder_all, grad_four)
     grad_three, gain_three, shift_three, _ = backward_layer(upstream, three, 2, own_loss, 6)
-    sample_grad = over_rows(lifting_all, grad_three)
+    sample_grad = over_rows(lifting_all, grad_three)[:plan.latent]
     center_grad = sample_grad + kl_weight * center
     logvar_grad = sample_grad * 0.5 * spread * draws + kl_weight * 0.5 * (jnp.exp(log_var) - 1.0)
     moment_grad = jnp.concatenate([center_grad, logvar_grad], axis=0).astype(jnp.bfloat16)
@@ -810,7 +996,7 @@
     encoder_part = over_cells(grad_two, one[0]).reshape(plan.hh, ny, plan.midp)
     decoder_part = over_cells(grad_four, three[0]).reshape(plan.hh, ny, plan.midp)
     projector_part = over_cells(two[0], moment_grad).reshape(plan.hh, ny, plan.moments)
-    lifting_part = over_cells(grad_three, sample)
+    lifting_part = over_cells(grad_three, sample)[:, :plan.latent]
 
     def lanes(value, width):
         return jnp.pad(value, ((0, 0), (0, 0), (0, width - value.shape[2])))

time: 852 us -> 749 us (0.88)
  other arithmetic: 75.5 us -> 34 us
  local copies, waits for them, and re-layouts: 91.3 us -> 65.9 us
  matrix products: 178 us -> 154 us
  Pallas kernels: 489 us -> 476 us
    pallas_call x8 -> x4, Pallas kernels: 89.4 us -> 45.2 us  [meet_all(): pl.pallas_call(functools.partial(meet_kernel, plan, merge), out_shape=jax...]
    pallas_call x1, Pallas kernels: 146 us -> 176 us  [forward_all(): pl.pallas_call(functools.partial(forward_kernel, plan, total_cells), out_...]
    dot_general x6 -> x2, matrix products: 49.9 us -> 26.4 us  [rows_dot(): lax.dot_general(left, right, (((1,), (0,)), ((), ())), preferred_element_...]
    reshape x7 -> x0, local copies, waits for them, and re-layouts: 15 us -> none  [the longest x4 6.8 us: spread_rows(): split = value.reshape(plan.nx, plan.h, *value.shape[1:])]
    convert_element_type x4 -> x0, other arithmetic: 12.3 us -> none  [forward_layer(): return (active.astype(jnp.bfloat16), normed, scaled, inverse)]
    unnamed x128 -> x71, local copies, waits for them, and re-layouts: 15.5 us -> 4.45 us
    convert_element_type x0 -> x2, local copies, waits for them, and re-layouts: none -> 10.1 us  [the longest x1 8.3 us: on_device(): small_part = jnp.concatenate([lanes(encoder_part, plan.midl), lanes(decod...]
    mul x4 -> x0, local copies, waits for them, and re-layouts: 8.82 us -> none  [forward_layer(): keeper = keepers[k].astype(jnp.float32) * keep_scale]
  transfers between devices with their start and end apart: 1 -> 1, of which waited for: 0 -> 0; matrix products, arithmetic and copies ran while one was open for 5% -> 1% of each run, Pallas kernels for 0% -> 0%
where the time goes in v2:
time: 749 us; the launch traced here: 737 us
  Pallas kernels  476 us (64%)
  matrix products  154 us (21%)
  local copies, waits for them, and re-layouts  65.9 us (9%)
  other arithmetic  34 us (5%)
    pallas_call x3, Pallas kernels, reduce_all(): pl.pallas_call(functools.partial(reduce_kernel, plan, width, factor), out...  246 us
    pallas_call x1, Pallas kernels, forward_all(): pl.pallas_call(functools.partial(forward_kernel, plan, total_cells), out_...  176 us
    dot_general x6, matrix products, over_rows(): lax.dot_general(left, right, (((0,), (0,)), ((), ())), preferred_element_...  84.6 us
    pallas_call x4, Pallas kernels, meet_all(): pl.pallas_call(functools.partial(meet_kernel, plan, merge), out_shape=jax...  45.2 us
    dot_general x6, matrix products, over_cells(): lax.dot_general(left, right, (((1,), (1,)), ((), ())), preferred_element_...  42.6 us
    dot_general x2, matrix products, rows_dot(): lax.dot_general(left, right, (((1,), (0,)), ((), ())), preferred_element_...  26.4 us
  transfers between devices with their start and end apart: 1, of which 0 were waited for; matrix products, arithmetic and copies ran while one was open for 1% of the time, Pallas kernels for 0%

profile of v2, /device:TPU:26, one launch (start us, length us, event | category | flops | bytes accessed | tf_op | source)
XLA Modules:
  0.0 737.0 jit_solution(5395135324754390116)
XLA Ops:
  11.8 175.8 %shard_map.263 = (bf16[896,7168]{1,0:T(8,128)(2,1)}, bf16[896,3072]{1,0:T(8,128)(2,1)}, bf16[896,7168]{1,0:T(8,128)(2,1)}, f32[100,768]{1,0:T(8,128)}, f32[100,7...) custom-call(bf16[112,1792]{1,0:T(8,128)(2,1)} %get-tuple-element.110, ...), custom_call_target="tpu_custom_call" | custom-call | tf_op jit(solution)/shard_map/pallas_call | solution.py:519
  187.6 7.9 %copy.82 = bf16[896,3072]{0,1:T(8,128)(2,1)} copy(bf16[896,3072]{1,0:T(8,128)(2,1)} %get-tuple-element.30) | data formatting | bytes 11010048 | tf_op jit(solution)/shard_map/reshape | solution.py:935
  203.3 19.5 %fusion.7 = f32[7000,768]{1,0:T(8,128)} fusion(bf16[896,7168]{1,0:T(8,128)(2,1)} %get-tuple-element.26, bf16[4,896,768]{2,1,0:T(8,128)(2,1)} %get-tuple-element.27), kind=kOutput, calls=%fused_computation.22 | convolution fusion | flops 9633792000 | bytes 35495936 | tf_op jit(solution)/shard_map/dot_general | solution.py:868
  222.9 21.5 %multiply_reduce_fusion = (f32[]{:T(128)}, bf16[7000,768]{1,0:T(8,128)(2,1)}, bf16[768,7000]{0,1:T(8,128)(2,1)}, f32[768,7000]{0,1:T(8,128)}) fusion(f32[7000,768]{1,0:T(8,128)} %fusion.7, bf16[768,7000]{0,1:T(8,128)(2,1)S(1)} %bitcast.215, s32[8,7000]{1,0:T(8,128)S(1)} %copy-done.12, s32[768]{0:T(1024)S(1)} %copy-done.13), kind=kOutput, calls=%fused_computation.6 | convolution fusion | flops 123710144 | bytes 75491072 | tf_op jit(solution)/shard_map/dot_general | solution.py:868
  244.4 17.5 %convolution_convert_fusion = bf16[896,7000]{1,0:T(8,128)(2,1)} fusion(bf16[7000,768]{1,0:T(8,128)(2,1)} %get-tuple-element.95, bf16[4,896,768]{2,1,0:T(8,128)(2,1)} %get-tuple-element.27), kind=kOutput, calls=%fused_computation.18 | convolution fusion | flops 9640064000 | bytes 24672256 | tf_op jit(solution)/shard_map/dot_general | solution.py:864
  262.6 20.9 %fusion.117 = (f32[896]{0:T(1024)S(1)}, f32[896]{0:T(1024)S(1)}, f32[896,768]{1,0:T(8,128)}) fusion(f32[4,896,768]{2,1,0:T(8,128)} %get-tuple-element.31, f32[896]{0:T(1024)S(1)} %get-tuple-element.84, f32[896]{0:T(1024)S(1)} %get-tuple-element.85, bf16[4,896,768]{2,1,0:T(8,128)(2,1)} %get-tuple-element.29, bf16[7000,768]{1,0:T(8,128)(2,1)} %get-tuple-element.95, ...), kind=kOutput, calls=%fused_computation.209 | convolution fusion | flops 9644111872 | bytes 30263296 | tf_op jit(solution)/shard_map/dot_general | solution.py:860
  286.3 12.0 %shard_map.264 = f32[3,896]{1,0:T(4,128)} custom-call(f32[3,896]{1,0:T(4,128)} %maximum_maximum_fusion.x_ref), custom_call_target="tpu_custom_call" | custom-call | tf_op jit(solution)/shard_map/pallas_call | solution.py:568
  302.4 6.5 fusion.116
  309.6 11.4 %shard_map.265 = f32[3,896]{1,0:T(4,128)} custom-call(f32[3,896]{1,0:T(4,128)} %maximum_maximum_fusion.1.x_ref), custom_call_target="tpu_custom_call" | custom-call | tf_op jit(solution)/shard_map/pallas_call | solution.py:568
  332.9 5.5 fusion.115
  339.1 11.5 %shard_map.266 = f32[3,896]{1,0:T(4,128)} custom-call(f32[3,896]{1,0:T(4,128)} %maximum_maximum_fusion.2.x_ref), custom_call_target="tpu_custom_call" | custom-call | tf_op jit(solution)/shard_map/pallas_call | solution.py:568
  366.4 8.3 %copy.79.x_ref = bf16[896,3072]{1,0:T(8,128)(2,1)} copy(bf16[896,3072]{0,1:T(8,128)(2,1)} %bitcast.216) | data formatting | bytes 11010048 | tf_op jit(solution)/shard_map/convert_element_type | solution.py:1008
  374.7 47.3 %shard_map.269 = f32[112,768]{1,0:T(8,128)} custom-call(bf16[896,3072]{1,0:T(8,128)(2,1)} %copy.79.x_ref), custom_call_target="tpu_custom_call" | custom-call | tf_op jit(solution)/shard_map/pallas_call | solution.py:840
  424.1 5.5 fusion.118
  429.7 5.7 pad_maximum_fusion.1.x_ref
  435.4 99.1 %shard_map.270 = f32[112,1920]{1,0:T(8,128)} custom-call(bf16[896,7680]{1,0:T(8,128)(2,1)} %pad_maximum_fusion.1.x_ref), custom_call_target="tpu_custom_call" | custom-call | tf_op jit(solution)/shard_map/pallas_call | solution.py:840
  536.0 8.5 %shard_map.271 = (f32[1,2048]{1,0:T(1,128)}, f32[112,128]{1,0:T(8,128)}) custom-call(f32[1,2048]{1,0:T(1,128)} %pad_maximum_fusion.4.row_ref, f32[112,128]{1,0:T(8,128)} %slice.276.block_ref), custom_call_target="tpu_custom_call" | custom-call | tf_op jit(solution)/shard_map/pallas_call | solution.py:605
  550.0 6.1 fusion.114
  556.7 10.3 %shard_map.267 = f32[3,896]{1,0:T(4,128)} custom-call(f32[3,896]{1,0:T(4,128)} %maximum_maximum_fusion.3.x_ref), custom_call_target="tpu_custom_call" | custom-call | tf_op jit(solution)/shard_map/pallas_call | solution.py:568
  572.4 17.6 %convolution_convert_fusion.1 = bf16[896,7000]{1,0:T(8,128)(2,1)} fusion(bf16[768,7000]{0,1:T(8,128)(2,1)} %param.16, f32[896,768]{1,0:T(8,128)} %get-tuple-element.127, f32[4,896,768]{2,1,0:T(8,128)} %get-tuple-element.31, f32[896]{0:T(1024)S(1)} %get-tuple-element.87, f32[896]{0:T(1024)S(1)} %get-tuple-element.86, f32[896]{0:T(1024)S(1)} %copy-done.22), kind=kOutput, calls=%fused_computation.19 | convolution fusion | flops 9644192768 | bytes 28811776 | tf_op jit(solution)/shard_map/dot_general | solution.py:864
  590.0 5.5 fusion.119
  595.5 5.7 pad_maximum_fusion.x_ref
  601.2 99.9 %shard_map.268 = f32[112,1920]{1,0:T(8,128)} custom-call(bf16[896,7680]{1,0:T(8,128)(2,1)} %pad_maximum_fusion.x_ref), custom_call_target="tpu_custom_call" | custom-call | tf_op jit(solution)/shard_map/pallas_call | solution.py:840
  704.6 29.0 %fusion.2 = bf16[768,7000]{0,1:T(8,128)(2,1)} fusion(f32[768,7000]{0,1:T(8,128)} %get-tuple-element.123, f32[7000,768]{1,0:T(8,128)} %fusion.7, bf16[768,7000]{0,1:T(8,128)(2,1)} %param.16, bf16[896,7168]{1,0:T(8,128)(2,1)} %get-tuple-element.34, f32[896,768]{1,0:T(8,128)} %get-tuple-element.127, f32[4,896,768]{2,1,0:T(8,128)} %get-tuple-element.31, ...), kind=kOutput, calls=%fused_computation.5 | convolution fusion | flops 9664800768 | bytes 82643456 | tf_op jit(solution)/shard_map/dot_general | solution.py:868
  (148 shorter events, 71.9 us)
Async XLA Ops:
  0.6 5.9 copy-start.27
  0.7 5.4 copy-start.15
  0.7 5.6 copy-start.25
  0.7 5.7 copy-start.26
  2.8 7.1 collective-permute-start
  201.6 21.3 %slice-start = ((s8[10752000]{0:T(1024)(128)(4,1)}), s8[4194304]{0:T(1024)(128)(4,1)S(1)}, s32[]{:S(2)}) async-start(s8[10752000]{0:T(1024)(128)(4,1)} %bitcast.214), calls=%async_computation | async-start | bytes 8388608
  203.3 19.6 %slice-start.1 = ((s8[10752000]{0:T(1024)(128)(4,1)}), s8[4194304]{0:T(1024)(128)(4,1)S(1)}, s32[]{:S(2)}) async-start(s8[10752000]{0:T(1024)(128)(4,1)} %bitcast.214), calls=%async_computation.1 | async-start | bytes 8388608
  203.3 19.6 %slice-start.2 = ((s8[10752000]{0:T(1024)(128)(4,1)}), s8[2363392]{0:T(1024)(128)(4,1)S(1)}, s32[]{:S(2)}) async-start(s8[10752000]{0:T(1024)(128)(4,1)} %bitcast.214), calls=%async_computation.2 | async-start | bytes 4726784
  203.3 19.6 %copy-start.12 = (s32[8,7000]{1,0:T(8,128)S(1)}, s32[8,7000]{1,0:T(8,128)}, u32[]{:S(2)}) copy-start(s32[8,7000]{1,0:T(8,128)} %param.18) | copy-start | bytes 672004
  203.3 19.6 %copy-start.13 = (s32[768]{0:T(1024)S(1)}, s32[768]{0:T(1024)}, u32[]{:S(2)}) copy-start(s32[768]{0:T(1024)} %param.17) | copy-start | bytes 9220
  244.4 17.5 %copy-start.21 = (f32[4,2,896]{2,1,0:T(2,128)S(1)}, f32[4,2,896]{2,1,0:T(2,128)}, u32[]{:S(2)}) copy-start(f32[4,2,896]{2,1,0:T(2,128)} %get-tuple-element.33) | copy-start | bytes 86020
  262.6 21.5 %copy-start.1 = (f32[100,768]{1,0:T(8,128)S(1)}, f32[100,768]{1,0:T(8,128)}, u32[]{:S(2)}) copy-start(f32[100,768]{1,0:T(8,128)} %get-tuple-element.28) | copy-start | bytes 921604
  262.6 21.6 %copy-start.10 = (f32[100,768]{1,0:T(8,128)S(1)}, f32[100,768]{1,0:T(8,128)}, u32[]{:S(2)}) copy-start(f32[100,768]{1,0:T(8,128)} %get-tuple-element.32) | copy-start | bytes 921604
  285.6 52.9 %copy-start.19 = (f32[3]{0:T(128)}, f32[3]{0:T(128)S(1)}, u32[]{:S(2)}) copy-start(f32[3]{0:T(128)S(1)} %pad.116.clone) | copy-start | bytes 40
  302.4 6.5 copy-start.7
  332.9 19.2 %copy-start.28 = (pred[128]{0:T(512)(128)(4,1)S(1)}, pred[128]{0:T(512)(128)(4,1)}, u32[]{:S(2)}) copy-start(pred[128]{0:T(512)(128)(4,1)} %constant.68.clone.1) | copy-start | bytes 388
  435.4 114.5 %copy-start.23 = (f32[896]{0:T(1024)S(1)}, f32[896]{0:T(1024)}, u32[]{:S(2)}) copy-start(f32[896]{0:T(1024)} %get-tuple-element.78) | copy-start | bytes 10756
  435.4 114.5 %copy-start.24 = (f32[896]{0:T(1024)S(1)}, f32[896]{0:T(1024)}, u32[]{:S(2)}) copy-start(f32[896]{0:T(1024)} %get-tuple-element.81) | copy-start | bytes 10756
  549.9 6.1 copy-start.20
  549.9 22.4 %copy-start.22 = (f32[896]{0:T(1024)S(1)}, f32[896]{0:T(1024)}, u32[]{:S(2)}) copy-start(f32[896]{0:T(1024)} %get-tuple-element.74) | copy-start | bytes 10756
  601.2 100.6 %copy-start = (f32[112,1920]{1,0:T(8,128)S(1)}, f32[112,1920]{1,0:T(8,128)}, u32[]{:S(2)}) copy-start(f32[112,1920]{1,0:T(8,128)} %shard_map.270) | copy-start | bytes 2580484
  704.6 29.7 %copy-start.16 = (f32[1,896]{1,0:T(1,128)S(1)}, f32[1,896]{1,0:T(1,128)}, u32[]{:S(2)}) copy-start(f32[1,896]{1,0:T(1,128)} %get-tuple-element.121) | copy-start | bytes 10756
  704.6 29.7 %copy-start.17 = (f32[1,896]{1,0:T(1,128)S(1)}, f32[1,896]{1,0:T(1,128)}, u32[]{:S(2)}) copy-start(f32[1,896]{1,0:T(1,128)} %get-tuple-element.116) | copy-start | bytes 10756
  704.6 29.7 %copy-start.18 = (f32[1,896]{1,0:T(1,128)S(1)}, f32[1,896]{1,0:T(1,128)}, u32[]{:S(2)}) copy-start(f32[1,896]{1,0:T(1,128)} %get-tuple-element.120) | copy-start | bytes 10756
  (9 other events, 30.1 us)

commit v3 on v2

--- a/solution.py
+++ b/solution.py
@@ -47,6 +47,7 @@
         self.blocks = nx * ny
         rows = round_up(self.hp * 2 // 3, 16)
         self.cuts = ((0, rows), (rows, self.hp - rows)) if rows < self.hp else ((0, rows),)
+        self.fits = self.blocks <= 32 and self.hh * ny * self.frame <= 7 * 1024 * 1024
 
 
 class Flow:
@@ -729,14 +730,22 @@
 
     def add_in(self, kind, cut, spot, stage, sign):
         own, twin, arrivals = self.gather_terms(kind, cut, spot, stage, sign)
-        own[...] = (own[...].astype(jnp.float32) + twin[...].astype(jnp.float32)).astype(jnp.bfloat16)
+
+        def add(other):
+            def chunk(i, _):
+                rows = aligned(i * 16, 16)
+                total = own[rows, :].astype(jnp.float32) + other[rows, :].astype(jnp.float32)
+                own[rows, :] = total.astype(jnp.bfloat16)
+                return 0
+            lax.fori_loop(0, cut[2] // 16, chunk, 0)
+
+        add(twin)
         for there, index in arrivals:
             slot, sem = self.slot(kind, index)
             @when(there)
             def _(slot=slot, sem=sem):
                 pltpu.make_async_copy(slot, slot, sem).wait()
-                own[...] = (own[...].astype(jnp.float32) + slot[...].astype(jnp.float32)).astype(
-                    jnp.bfloat16)
+                add(slot)
         return own
 
     def onward(self, kind, cut, spot, stage, sign):
@@ -770,40 +779,43 @@
     def toward(self, flow, axis, sign):
         return flow.step(axis, sign)
 
-    def walk(self, visit, stage):
-        for kind, cut in enumerate(self.cuts):
-            flow = cut[0]
-            p, q, r = flow.here
-            np_, nq, nr = flow.limit
-            mp, mq, mr = flow.most
-
-            def one(n, _, kind=kind, cut=cut):
+    def order(self, kind):
+        most = self.cuts[kind][0].most
+        return [(stage, k) for stage in (2, 1, 0) for k in range(most[stage] - 1, 0, -1)]
+
+    def steps(self):
+        return max(len(self.order(kind)) for kind in range(len(self.cuts)))
+
+    def walk(self, visit, kind, stage, k):
+        cut = self.cuts[kind]
+        p, q, r = cut[0].here
+        np_, nq, nr = cut[0].limit
+        mp, mq, mr = cut[0].most
+
+        def one(n, _):
+            dp, dq = lax.rem(n, mp), n // mp
+            for sign in (-1, 1):
                 if stage == 2:
-                    k, dq, dp = mr - 1 - n // (mq * mp), lax.rem(n // mp, mq), lax.rem(n, mp)
+                    d = r + sign * k
+                    spot, good = (dp, dq, d), (d >= 0) & (d < nr) & (dq < nq) & (dp < np_)
                 elif stage == 1:
-                    k, dp = mq - 1 - n // mp, lax.rem(n, mp)
+                    d = q + sign * k
+                    spot, good = (dp, d, r), (d >= 0) & (d < nq) & (dp < np_)
                 else:
-                    k = mp - 1 - n
-                for sign in (-1, 1):
-                    if stage == 2:
-                        d = r + sign * k
-                        spot, good = (dp, dq, d), (d >= 0) & (d < nr) & (dq < nq) & (dp < np_)
-                    elif stage == 1:
-                        d = q + sign * k
-                        spot, good = (dp, d, r), (d >= 0) & (d < nq) & (dp < np_)
-                    else:
-                        d = p + sign * k
-                        spot, good = (d, q, r), (d >= 0) & (d < np_)
-                    pl.when(good)(functools.partial(visit, kind, cut, spot, stage, sign))
-                return 0
-            count = {2: (mr - 1) * mq * mp, 1: (mq - 1) * mp, 0: mp - 1}[stage]
-            lax.fori_loop(0, count, one, 0)
-
-    def pass_on(self, stage):
+                    d = p + sign * k
+                    spot, good = (d, q, r), (d >= 0) & (d < np_)
+                pl.when(good)(functools.partial(visit, kind, cut, spot, stage, sign))
+            return 0
+        lax.fori_loop(0, {2: mq * mp, 1: mp, 0: 1}[stage], one, 0)
+
+    def pass_on(self, step):
         def visit(kind, cut, spot, stage, sign):
             self.add_in(kind, cut, spot, stage, sign)
             self.onward(kind, cut, spot, stage, sign).start()
-        self.walk(visit, stage)
+        for kind in range(len(self.cuts)):
+            order = self.order(kind)
+            if step < len(order):
+                self.walk(visit, kind, *order[step])
 
     def own_sum(self, out_ref, factor):
         for kind, cut in enumerate(self.cuts):
@@ -815,45 +827,348 @@
         self.each_twin(lambda copy: copy.wait_send())
         def visit(kind, cut, spot, stage, sign):
             self.onward(kind, cut, spot, stage, sign).wait_send()
-        for stage in (2, 1, 0):
-            self.walk(visit, stage)
-
-
-def reduce_kernel(plan, width, factor, x_ref, o_ref, part, twin, *rest):
+        for kind in range(len(self.cuts)):
+            for stage, k in self.order(kind):
+                self.walk(visit, kind, stage, k)
+
+    def twin_column(self, gy):
+        y, flow = gy // 2, self.cuts[0][0]
+
+        @pl.when(gy % 2 != flow.core)
+        def _():
+            for kind, cut in enumerate(self.cuts):
+                def one(gx, _, kind=kind, cut=cut):
+                    self.twin_copy(kind, cut, gx, y).start()
+                    return 0
+                lax.fori_loop(0, self.plan.nx, one, 0)
+
+
+def reduce_scratch(plan, width):
+    counts = [sum(c) for c in Reduce.slot_counts(plan)]
+    return [
+        pltpu.VMEM((plan.hh, plan.ny * width), jnp.bfloat16),
+        pltpu.VMEM((plan.hh, plan.ny // 2 * width), jnp.bfloat16),
+        *[pltpu.VMEM((c, cut[1], width), jnp.bfloat16) for c, cut in zip(counts, plan.cuts)],
+        pltpu.SemaphoreType.DMA((len(plan.cuts), plan.blocks // 2)),
+        pltpu.SemaphoreType.DMA((2, len(plan.cuts), plan.blocks // 2)),
+        *[pltpu.SemaphoreType.DMA((c,)) for c in counts],
+    ]
+
+
+def reduce_from(plan, width, refs):
     n = len(plan.cuts)
-    slots, (send_sem, twin_sem), recv_sem, load_sem = rest[:n], rest[n:n + 2], rest[n + 2:2 * n + 2], rest[-1]
-    load = pltpu.make_async_copy(x_ref, part, load_sem)
+    part, twin, slots, sems, recv = refs[0], refs[1], refs[2:2 + n], refs[2 + n:4 + n], refs[4 + n:]
+    return Reduce(plan, width, part, twin, slots, *sems, recv)
+
+
+def reduce_kernel(plan, width, factor, x_ref, o_ref, *rest):
+    reduce = reduce_from(plan, width, rest[:-1])
+    load = pltpu.make_async_copy(x_ref, reduce.part, rest[-1])
     load.start()
     greet(plan)
     load.wait()
-    reduce = Reduce(plan, width, part, twin, slots, send_sem, twin_sem, recv_sem)
     reduce.start_twin()
-    for stage in (2, 1, 0):
-        reduce.pass_on(stage)
+    for step in range(reduce.steps()):
+        reduce.pass_on(step)
     reduce.own_sum(o_ref, factor)
     reduce.finish_sends()
 
 
 def reduce_all(plan, value, factor, collective_id):
     width = value.shape[1] // plan.ny
-    counts = [sum(c) for c in Reduce.slot_counts(plan)]
     return pl.pallas_call(
         functools.partial(reduce_kernel, plan, width, factor),
         out_shape=jax.ShapeDtypeStruct((plan.hp, width), jnp.float32),
         in_specs=[pl.BlockSpec(memory_space=pl.ANY)],
         out_specs=pl.BlockSpec(memory_space=pltpu.VMEM),
-        scratch_shapes=[
-            pltpu.VMEM((plan.hh, plan.ny * width), jnp.bfloat16),
-            pltpu.VMEM((plan.hh, plan.ny // 2 * width), jnp.bfloat16),
-            *[pltpu.VMEM((c, cut[1], width), jnp.bfloat16) for c, cut in zip(counts, plan.cuts)],
-            pltpu.SemaphoreType.DMA((len(plan.cuts), plan.blocks // 2)),
-            pltpu.SemaphoreType.DMA((2, len(plan.cuts), plan.blocks // 2)),
-            *[pltpu.SemaphoreType.DMA((c,)) for c in counts],
-            pltpu.SemaphoreType.DMA,
-        ],
+        scratch_shapes=[*reduce_scratch(plan, width), pltpu.SemaphoreType.DMA],
         compiler_params=pltpu.CompilerParams(
             collective_id=collective_id, has_side_effects=True, vmem_limit_bytes=60 * 1024 * 1024),
     )(value)
+
+
+def backward_kernel(plan, total_cells, *refs):
+    (part_hbm, up_hbm, small_hbm, layers_hbm, scaled_hbm, keep_hbm, sample_ref, rows_ref, loss_ref,
+     center_ref, log_var_ref, draws_ref,
+     readout_out, sums_out, small_part, grad_ref,
+     small_ref, up_ref, layer_ref, scaled_ref, keep_ref, lane_ref, column_ref, latent_ref,
+     moment_ref, wide, tall, meet_send, meet_recv, load_sem, *rest) = refs
+    reduce = reduce_from(plan, plan.frame, rest)
+
+    def load(k):
+        slot = k % 2
+        return (
+            pltpu.make_async_copy(scaled_hbm.at[k], scaled_ref.at[slot], load_sem.at[3 * slot]),
+            pltpu.make_async_copy(keep_hbm.at[k], keep_ref.at[slot], load_sem.at[3 * slot + 1]),
+        )
+
+    def load_layer(k):
+        return pltpu.make_async_copy(
+            layers_hbm.at[k], layer_ref.at[k % 2, pl.ds(0, plan.hh), :], load_sem.at[3 * (k % 2) + 2])
+
+    first = pltpu.make_async_copy(part_hbm, reduce.part, load_sem.at[6])
+    second = pltpu.make_async_copy(up_hbm, up_ref, load_sem.at[7])
+    third = pltpu.make_async_copy(small_hbm, small_ref, load_sem.at[8])
+    first.start()
+    second.start()
+    for copy in load(3):
+        copy.start()
+    third.start()
+    load_layer(2).start()
+    for copy in load(2):
+        copy.start()
+    load_layer(1).start()
+    peers = Meet.peers(plan)
+    barrier = pltpu.get_barrier_semaphore()
+    for device in peers:
+        pl.semaphore_signal(barrier, inc=1, device_id=device, device_id_type=MESH)
+    pl.semaphore_wait(barrier, len(peers))
+    first.wait()
+    reduce.start_twin()
+    tail = layer_ref.shape[1] - plan.hh
+    if tail:
+        for k in range(2):
+            layer_ref[k, plan.hh:, :] = jnp.zeros((tail, plan.cells), jnp.bfloat16)
+    latent_ref[...] = jnp.zeros_like(latent_ref)
+
+    todo = [functools.partial(reduce.pass_on, step) for step in range(reduce.steps())]
+    todo.append(lambda: reduce.own_sum(readout_out, 1.0 / total_cells))
+
+    def between(second):
+        if todo:
+            todo.pop(0)()
+
+    def layer(k):
+        slot = k % 2
+        for copy in load(k):
+            copy.wait()
+
+        def columns(i):
+            column_ref[0] = unit_column(plan, small_ref, i, plan.latent + k)
+            column_ref[1] = unit_column(plan, small_ref, i, plan.latent + 4 + k)
+            column_ref[2] = as_column(
+                lax.rsqrt(rows_ref[k, 1:2, aligned(i * LANES)] / total_cells + norm_eps))
+
+        def block(i, _):
+            columns(i)
+
+            def chunk(j, _):
+                rows = aligned(i * LANES + j * 16, 16)
+                here = aligned(j * 16, 16)
+                gain, bias = tiled(column_ref[0, here, :], plan), tiled(column_ref[1, here, :], plan)
+                scaled = scaled_ref[slot, rows, :]
+                normed = gain * scaled + bias
+                sigma = jax.nn.sigmoid(normed)
+                slope = up_ref[rows, :] * keep_ref[slot, rows, :].astype(jnp.float32) * sigma * (
+                    1.0 + normed * (1.0 - sigma))
+                up_ref[rows, :] = slope
+                lane_ref[0, here, :] = lane_sums(slope)
+                lane_ref[1, here, :] = lane_sums(slope * scaled)
+                return 0
+            lax.fori_loop(0, LANES // 16, chunk, 0)
+            sums_out[k, 0:1, aligned(i * LANES)] = as_row(lane_ref[0])
+            sums_out[k, 1:2, aligned(i * LANES)] = as_row(lane_ref[1])
+            return 0
+        lax.fori_loop(0, plan.hh // LANES, block, 0)
+        sums_out[k, 2:3, :] = loss_ref[...]
+        meet = Meet(plan, wide.at[k], tall.at[k], meet_send.at[k], meet_recv.at[k])
+        sums_out[k] = meet.run(sums_out[k], merge_sums, 1.0, between)
+
+        def last(i, _):
+            columns(i)
+            column_ref[3] = as_column(sums_out[k, 0:1, aligned(i * LANES)] / total_cells)
+            column_ref[4] = as_column(sums_out[k, 1:2, aligned(i * LANES)] / total_cells)
+
+            def chunk(j, _):
+                rows = aligned(i * LANES + j * 16, 16)
+                here = aligned(j * 16, 16)
+                factor = tiled(column_ref[0, here, :] * column_ref[2, here, :], plan)
+                shift, gain = tiled(column_ref[3, here, :], plan), tiled(column_ref[4, here, :], plan)
+                grad = factor * (up_ref[rows, :] - (shift + scaled_ref[slot, rows, :] * gain))
+                grad_ref[rows, :] = grad.astype(jnp.bfloat16)
+                return 0
+            lax.fori_loop(0, LANES // 16, chunk, 0)
+            return 0
+        lax.fori_loop(0, plan.hh // LANES, last, 0)
+        if k >= 2:
+            for copy in load(k - 2):
+                copy.start()
+
+    def put(j, lane, value):
+        at = j * plan.small + lane
+        small_part[:, at:at + value.shape[1]] = value.astype(jnp.bfloat16)
+
+    def middle(source, lane):
+        for j in range(plan.ny):
+            at, row = j * plan.small + lane, j * plan.midp
+            put(j, lane, over_cells(grad_ref[...], source[row:row + plan.midl, :]))
+            up_ref[row:row + plan.midp, :] = over_rows(
+                small_ref[:, at:at + plan.midl], grad_ref[...])[:plan.midp]
+
+    second.wait()
+    third.wait()
+    layer(3)
+    load_layer(2).wait()
+    middle(layer_ref.at[0], plan.o4)
+    load_layer(0).start()
+    layer(2)
+    lifting = over_cells(grad_ref[...], sample_ref[...])
+    for j in range(plan.ny):
+        put(j, plan.ol, lifting)
+    reach = over_rows(small_ref[:, plan.ol:plan.ol + plan.ll], grad_ref[...])[:plan.latent]
+    center, log_var = center_ref[...], log_var_ref[...]
+    latent_ref[0, 0:plan.latent, :] = reach + kl_weight * center
+    latent_ref[1, 0:plan.latent, :] = (
+        reach * 0.5 * jnp.exp(0.5 * log_var) * draws_ref[...]
+        + kl_weight * 0.5 * (jnp.exp(log_var) - 1.0))
+    half, tall_rows = plan.ny // 2, round_up(plan.moments, 16)
+    moment_ref[...] = jnp.zeros_like(moment_ref)
+    for j in range(plan.ny):
+        spot = (j % half) * plan.moments
+        piece = latent_ref[j // half, spot:spot + tall_rows, :]
+        row = lax.broadcasted_iota(jnp.int32, piece.shape, 0)
+        piece = jnp.where(row < plan.moments, piece, 0.0)
+        moment_ref[j * plan.ml:j * plan.ml + tall_rows, :] = piece.astype(jnp.bfloat16)
+    load_layer(1).wait()
+    for j in range(plan.ny):
+        at, row = j * plan.small + plan.op, j * plan.ml
+        moments = moment_ref[row:row + plan.ml, :]
+        put(j, plan.op, over_cells(layer_ref[1, 0:plan.hh, :], moments))
+        part = rows_dot(small_ref[:, at:at + plan.ml], moments)
+        up_ref[...] = part if j == 0 else up_ref[...] + part
+    layer(1)
+    load_layer(0).wait()
+    middle(layer_ref.at[0], plan.o2)
+    layer(0)
+    while todo:
+        between(False)
+    reduce.finish_sends()
+
+
+def backward_all(plan, total_cells, *arrays):
+    any_spec, vmem = pl.BlockSpec(memory_space=pl.ANY), pl.BlockSpec(memory_space=pltpu.VMEM)
+    f32, bf16 = jnp.float32, jnp.bfloat16
+    n = plan.nx + plan.ny - 2
+    shape = jax.ShapeDtypeStruct
+    return pl.pallas_call(
+        functools.partial(backward_kernel, plan, total_cells),
+        out_shape=[
+            shape((plan.hp, plan.frame), f32), shape((4, 3, plan.hh), f32),
+            shape((plan.hh, plan.ny * plan.small), bf16), shape((plan.hh, plan.cells), bf16)],
+        in_specs=[any_spec] * 6 + [vmem] * 6,
+        out_specs=[vmem] * 4,
+        scratch_shapes=[
+            pltpu.VMEM((plan.hh, plan.ny * plan.small), bf16),
+            pltpu.VMEM((plan.hh, plan.cells), f32),
+            pltpu.VMEM((2, plan.hh + plan.midl - plan.midp, plan.cells), bf16),
+            pltpu.VMEM((2, plan.hh, plan.cells), f32),
+            pltpu.VMEM((2, plan.hh, plan.cells), bf16),
+            pltpu.VMEM((2, LANES, LANES), f32),
+            pltpu.VMEM((5, LANES, LANES), f32),
+            pltpu.VMEM((2, plan.ll, plan.cells), f32),
+            pltpu.VMEM((plan.ny * plan.ml, plan.cells), bf16),
+            pltpu.VMEM((4, plan.nx, 3, plan.hh), f32),
+            pltpu.VMEM((4, plan.ny, 3, plan.hh), f32),
+            pltpu.SemaphoreType.DMA((4, n)),
+            pltpu.SemaphoreType.DMA((4, n)),
+            pltpu.SemaphoreType.DMA((9,)),
+            *reduce_scratch(plan, plan.frame),
+        ],
+        compiler_params=pltpu.CompilerParams(
+            collective_id=6, has_side_effects=True, vmem_limit_bytes=60 * 1024 * 1024),
+    )(*arrays)
+
+
+def embed_kernel(plan, total_cells, *refs):
+    (small_hbm, x_hbm, grad_ref, readout_ref, embed_out, small_out, row_out, block_out,
+     x_ref, wide, tall, meet_send, meet_recv, load_sem, *rest) = refs
+    half = len(rest) // 2
+    small, embed = reduce_from(plan, plan.small, rest[:half]), reduce_from(plan, plan.frame, rest[half:])
+    first = pltpu.make_async_copy(small_hbm, small.part, load_sem.at[0])
+    second = pltpu.make_async_copy(x_hbm, x_ref, load_sem.at[1])
+    first.start()
+    second.start()
+    peers = Meet.peers(plan)
+    barrier = pltpu.get_barrier_semaphore()
+    for device in peers:
+        pl.semaphore_signal(barrier, inc=1, device_id=device, device_id_type=MESH)
+    pl.semaphore_wait(barrier, len(peers))
+    first.wait()
+    small.start_twin()
+    second.wait()
+    factor = 1.0 / total_cells
+    piece = plan.frame // 3 // LANES * LANES
+    for j in range(plan.ny):
+        start, stop = plan.frame_start[j], min(plan.frame_start[j] + plan.frame, plan.genes)
+        for at in range(start, stop, piece):
+            end = min(at + piece, stop)
+            to = j * plan.frame + at - start
+            embed.part[:, to:to + end - at] = over_cells(
+                grad_ref[...], x_ref[at:end, :]).astype(jnp.bfloat16)
+        done = stop - start
+        if done < plan.frame:
+            inside = done // LANES * LANES
+            lanes = lax.broadcasted_iota(jnp.int32, (plan.hh, LANES), 1)
+            at = j * plan.frame + inside
+            if inside < done:
+                value = embed.part[:, at:at + LANES]
+                embed.part[:, at:at + LANES] = jnp.where(
+                    lanes < done - inside, value.astype(jnp.float32), 0.0).astype(jnp.bfloat16)
+                inside += LANES
+            for at in range(j * plan.frame + inside, (j + 1) * plan.frame, LANES):
+                embed.part[:, at:at + LANES] = jnp.zeros((plan.hh, LANES), jnp.bfloat16)
+        embed.twin_column(j)
+        if j < small.steps():
+            small.pass_on(j)
+    for step in range(plan.ny, small.steps()):
+        small.pass_on(step)
+    embed.pass_on(0)
+    small.own_sum(small_out, factor)
+    meet = Meet(plan, wide, tall, meet_send, meet_recv)
+    wide[meet.gx, :, 0:plan.frame] = readout_ref[...]
+    wide[meet.gx, :, plan.frame:] = small_out[plan.h:plan.h + 1, plan.op:plan.op + plan.ml]
+    tall[meet.gy] = small_out[:, plan.ol:plan.ol + plan.ll]
+    copies = meet.copies(False) + meet.copies(True)
+    for copy in copies:
+        copy.start()
+    for step in range(1, embed.steps()):
+        embed.pass_on(step)
+    for copy in copies:
+        copy.wait_recv()
+    row_out[...] = wide[0]
+    block_out[...] = tall[0]
+    embed.own_sum(embed_out, factor)
+    for copy in copies:
+        copy.wait_send()
+    small.finish_sends()
+    embed.finish_sends()
+
+
+def embed_all_sums(plan, total_cells, *arrays):
+    any_spec, vmem = pl.BlockSpec(memory_space=pl.ANY), pl.BlockSpec(memory_space=pltpu.VMEM)
+    f32, bf16 = jnp.float32, jnp.bfloat16
+    n = plan.nx + plan.ny - 2
+    shape = jax.ShapeDtypeStruct
+    row, block = (1, plan.frame + plan.ml), (plan.hp, plan.ll)
+    return pl.pallas_call(
+        functools.partial(embed_kernel, plan, total_cells),
+        out_shape=[shape((plan.hp, plan.frame), f32), shape((plan.hp, plan.small), f32),
+                   shape(row, f32), shape(block, f32)],
+        in_specs=[any_spec] * 2 + [vmem] * 2,
+        out_specs=[vmem] * 4,
+        scratch_shapes=[
+            pltpu.VMEM((plan.genes, plan.cells), bf16),
+            pltpu.VMEM((plan.nx, *row), f32),
+            pltpu.VMEM((plan.ny, *block), f32),
+            pltpu.SemaphoreType.DMA((n,)),
+            pltpu.SemaphoreType.DMA((n,)),
+            pltpu.SemaphoreType.DMA((2,)),
+            *reduce_scratch(plan, plan.small),
+            *reduce_scratch(plan, plan.frame),
+        ],
+        compiler_params=pltpu.CompilerParams(
+            collective_id=7, has_side_effects=True, vmem_limit_bytes=60 * 1024 * 1024),
+    )(*arrays)
 
 
 def rows_dot(left, right):
@@ -932,37 +1247,7 @@
      norm_rows) = forward_all(
         plan, total_cells, wide[:plan.hp], small, wide[plan.hp:], profiles,
         jnp.swapaxes(retained_unit_flags, 1, 2), draws)
-    parts = small_all.reshape(plan.hh, ny, plan.small)
-    encoder_all = parts[:, :, plan.o2:plan.o2 + plan.midp].reshape(plan.hh, plan.hh)
-    decoder_all = parts[:, :, plan.o4:plan.o4 + plan.midp].reshape(plan.hh, plan.hh)
-    projector_all = parts[:, :, plan.op:plan.op + plan.moments].reshape(plan.hh, 2 * plan.latent)
-    lifting_all = parts[:, 0, plan.ol:plan.ol + plan.latent]
-    rows = parts[:, 0, plan.ol + plan.latent:plan.ol + plan.latent + 8].astype(jnp.float32)
-    gains = [rows[:, k:k + 1] for k in range(4)]
-    biases = [rows[:, 4 + k:5 + k] for k in range(4)]
-
-    spread = jnp.exp(0.5 * log_var)
-
-    def kept_layer(k):
-        inverse = lax.rsqrt(norm_rows[k, 1] / total_cells + norm_eps)[:, None]
-        return layers[k], gains[k] * scaled_values[k] + biases[k], scaled_values[k], inverse
-
-    one, two, three, four = (kept_layer(k) for k in range(4))
-
-    def backward_layer(upstream, kept, k, loss, ident):
-        _, normed, scaled, inverse = kept
-        sigma = jax.nn.sigmoid(normed)
-        slope = upstream * keep_values[k].astype(jnp.float32) * sigma * (
-            1.0 + normed * (1.0 - sigma))
-        pair = jnp.stack([jnp.sum(slope, axis=1), jnp.sum(slope * scaled, axis=1),
-                          jnp.full((plan.hh,), loss)])
-        merged = meet_all(plan, pair, merge_sums, 2)
-        shift, gain = merged[0], merged[1]
-        grad = gains[k] * inverse * (
-            slope - (shift[:, None] + scaled * gain[:, None]) / total_cells)
-        return grad.astype(jnp.bfloat16), gain, shift, merged[2, 0]
-
-    output = over_rows(readout_all[:, :plan.genes], four[0])
+    output = over_rows(readout_all[:, :plan.genes], layers[3])
     residual = output - profiles.astype(jnp.float32)
     picker = (jnp.arange(measured_flags.shape[0], dtype=jnp.int32)[:, None]
               == experiment_labels[None, :]).astype(jnp.bfloat16)
@@ -978,47 +1263,88 @@
         return jnp.concatenate(
             [padded[:, s:s + plan.frame] for s in plan.frame_start], axis=1).astype(jnp.bfloat16)
 
-    readout_part = frames(over_cells(four[0], output_grad))
+    readout_part = frames(over_cells(layers[3], output_grad))
     upstream = rows_dot(readout_all[:, :plan.genes], output_grad)
-    grad_four, gain_four, shift_four, loss_sum = backward_layer(upstream, four, 3, own_loss, 5)
-    upstream = over_rows(decoder_all, grad_four)
-    grad_three, gain_three, shift_three, _ = backward_layer(upstream, three, 2, own_loss, 6)
-    sample_grad = over_rows(lifting_all, grad_three)[:plan.latent]
-    center_grad = sample_grad + kl_weight * center
-    logvar_grad = sample_grad * 0.5 * spread * draws + kl_weight * 0.5 * (jnp.exp(log_var) - 1.0)
-    moment_grad = jnp.concatenate([center_grad, logvar_grad], axis=0).astype(jnp.bfloat16)
-    upstream = rows_dot(projector_all, moment_grad)
-    grad_two, gain_two, shift_two, _ = backward_layer(upstream, two, 1, own_loss, 7)
-    upstream = over_rows(encoder_all, grad_two)
-    grad_one, gain_one, shift_one, _ = backward_layer(upstream, one, 0, own_loss, 8)
+    if plan.fits:
+        readout_sum, sums, small_part, grad_one = backward_all(
+            plan, total_cells, readout_part, upstream, small_all, layers, scaled_values, keep_values,
+            sample, norm_rows, jnp.full((1, plan.hh), own_loss), center, log_var, draws)
+        loss_sum = sums[0, 2, 0]
+        gains_sum, shifts_sum = [sums[k, 1] for k in range(4)], [sums[k, 0] for k in range(4)]
+        embed_sum, small_sum, row, lifting_own = embed_all_sums(
+            plan, total_cells, small_part, profiles, grad_one, readout_sum[plan.h:plan.h + 1])
+    else:
+        parts = small_all.reshape(plan.hh, ny, plan.small)
+        encoder_all = parts[:, :, plan.o2:plan.o2 + plan.midp].reshape(plan.hh, plan.hh)
+        decoder_all = parts[:, :, plan.o4:plan.o4 + plan.midp].reshape(plan.hh, plan.hh)
+        projector_all = parts[:, :, plan.op:plan.op + plan.moments].reshape(plan.hh, 2 * plan.latent)
+        lifting_all = parts[:, 0, plan.ol:plan.ol + plan.latent]
+        rows = parts[:, 0, plan.ol + plan.latent:plan.ol + plan.latent + 8].astype(jnp.float32)
+        gains = [rows[:, k:k + 1] for k in range(4)]
+        biases = [rows[:, 4 + k:5 + k] for k in range(4)]
+
+        spread = jnp.exp(0.5 * log_var)
+
+        def kept_layer(k):
+            inverse = lax.rsqrt(norm_rows[k, 1] / total_cells + norm_eps)[:, None]
+            return layers[k], gains[k] * scaled_values[k] + biases[k], scaled_values[k], inverse
+
+        one, two, three, four = (kept_layer(k) for k in range(4))
+
+        def backward_layer(upstream, kept, k, loss, ident):
+            _, normed, scaled, inverse = kept
+            sigma = jax.nn.sigmoid(normed)
+            slope = upstream * keep_values[k].astype(jnp.float32) * sigma * (
+                1.0 + normed * (1.0 - sigma))
+            pair = jnp.stack([jnp.sum(slope, axis=1), jnp.sum(slope * scaled, axis=1),
+                              jnp.full((plan.hh,), loss)])
+            merged = meet_all(plan, pair, merge_sums, 2)
+            shift, gain = merged[0], merged[1]
+            grad = gains[k] * inverse * (
+                slope - (shift[:, None] + scaled * gain[:, None]) / total_cells)
+            return grad.astype(jnp.bfloat16), gain, shift, merged[2, 0]
+
+        grad_four, gain_four, shift_four, loss_sum = backward_layer(upstream, four, 3, own_loss, 5)
+        upstream = over_rows(decoder_all, grad_four)
+        grad_three, gain_three, shift_three, _ = backward_layer(upstream, three, 2, own_loss, 6)
+        sample_grad = over_rows(lifting_all, grad_three)[:plan.latent]
+        center_grad = sample_grad + kl_weight * center
+        logvar_grad = sample_grad * 0.5 * spread * draws + kl_weight * 0.5 * (jnp.exp(log_var) - 1.0)
+        moment_grad = jnp.concatenate([center_grad, logvar_grad], axis=0).astype(jnp.bfloat16)
+        upstream = rows_dot(projector_all, moment_grad)
+        grad_two, gain_two, shift_two, _ = backward_layer(upstream, two, 1, own_loss, 7)
+        upstream = over_rows(encoder_all, grad_two)
+        grad_one, gain_one, shift_one, _ = backward_layer(upstream, one, 0, own_loss, 8)
+        gains_sum = [gain_one, gain_two, gain_three, gain_four]
+        shifts_sum = [shift_one, shift_two, shift_three, shift_four]
+        encoder_part = over_cells(grad_two, one[0]).reshape(plan.hh, ny, plan.midp)
+        decoder_part = over_cells(grad_four, three[0]).reshape(plan.hh, ny, plan.midp)
+        projector_part = over_cells(two[0], moment_grad).reshape(plan.hh, ny, plan.moments)
+        lifting_part = over_cells(grad_three, sample)[:, :plan.latent]
+
+        def lanes(value, width):
+            return jnp.pad(value, ((0, 0), (0, 0), (0, width - value.shape[2])))
+
+        small_part = jnp.concatenate([
+            lanes(encoder_part, plan.midl), lanes(decoder_part, plan.midl),
+            lanes(projector_part, plan.ml),
+            jnp.broadcast_to(pad_to(lifting_part, plan.hh, plan.ll)[:, None, :], (plan.hh, ny, plan.ll)),
+        ], axis=2).reshape(plan.hh, ny * plan.small).astype(jnp.bfloat16)
+        embed_part = frames(over_cells(grad_one, profiles))
+
+        readout_sum = reduce_all(plan, readout_part, 1.0 / total_cells, 3)
+        small_sum = reduce_all(plan, small_part, 1.0 / total_cells, 4)
+        embed_sum = reduce_all(plan, embed_part, 1.0 / total_cells, 3)
+
+        row, lifting_own = share_all(plan, jnp.concatenate([
+            readout_sum[plan.h:plan.h + 1],
+            small_sum[plan.h:plan.h + 1, plan.op:plan.op + plan.ml]], axis=1),
+            small_sum[:, plan.ol:plan.ol + plan.ll], 5)
     input_grad = (over_rows(embed_all[:, :plan.genes], grad_one) - weighted).astype(jnp.bfloat16)
 
-    encoder_part = over_cells(grad_two, one[0]).reshape(plan.hh, ny, plan.midp)
-    decoder_part = over_cells(grad_four, three[0]).reshape(plan.hh, ny, plan.midp)
-    projector_part = over_cells(two[0], moment_grad).reshape(plan.hh, ny, plan.moments)
-    lifting_part = over_cells(grad_three, sample)[:, :plan.latent]
-
-    def lanes(value, width):
-        return jnp.pad(value, ((0, 0), (0, 0), (0, width - value.shape[2])))
-
-    small_part = jnp.concatenate([
-        lanes(encoder_part, plan.midl), lanes(decoder_part, plan.midl),
-        lanes(projector_part, plan.ml),
-        jnp.broadcast_to(pad_to(lifting_part, plan.hh, plan.ll)[:, None, :], (plan.hh, ny, plan.ll)),
-    ], axis=2).reshape(plan.hh, ny * plan.small).astype(jnp.bfloat16)
-    embed_part = frames(over_cells(grad_one, profiles))
-
-    readout_sum = reduce_all(plan, readout_part, 1.0 / total_cells, 3)
-    small_sum = reduce_all(plan, small_part, 1.0 / total_cells, 4)
-    embed_sum = reduce_all(plan, embed_part, 1.0 / total_cells, 3)
     starts = jnp.array([plan.g * j - plan.frame_start[j] for j in range(ny)], jnp.int32)
     readout_own = lax.dynamic_slice_in_dim(readout_sum, starts[gy], plan.g, 1)
     embed_own = lax.dynamic_slice_in_dim(embed_sum, starts[gy], plan.g, 1)
-
-    row, lifting_own = share_all(plan, jnp.concatenate([
-        readout_sum[plan.h:plan.h + 1],
-        small_sum[plan.h:plan.h + 1, plan.op:plan.op + plan.ml]], axis=1),
-        small_sum[:, plan.ol:plan.ol + plan.ll], 5)
     baseline_own = lax.dynamic_slice_in_dim(row[0, :plan.frame], starts[gy], plan.g, 0)
 
     def own_units(values):
@@ -1039,8 +1365,8 @@
         middle_back(plan, small_sum[:, plan.o4:plan.o4 + plan.midl]),
         readout_own[:plan.h],
         baseline_own,
-        own_units([gain_one, gain_two, gain_three, gain_four]),
-        own_units([shift_one, shift_two, shift_three, shift_four]),
+        own_units(gains_sum),
+        own_units(shifts_sum),
     )
 
 

time: 749 us -> 615 us (0.82)
  the two profiles are of different devices: /device:TPU:26 before, /device:TPU:11 now
where the time goes in v3:
time: 615 us; the launch traced here: 604 us
  Pallas kernels  443 us (72%)
  matrix products  105 us (17%)
  local copies, waits for them, and re-layouts  31.8 us (5%)
  other arithmetic  16 us (3%)
  between operations  6.15 us (1%)
    pallas_call x1, Pallas kernels, forward_all(): pl.pallas_call(functools.partial(forward_kernel, plan, total_cells), out_...  177 us
    pallas_call x1, Pallas kernels, embed_all_sums(): pl.pallas_call(functools.partial(embed_kernel, plan, total_cells), out_sh...  136 us
    pallas_call x1, Pallas kernels, backward_all(): pl.pallas_call(functools.partial(backward_kernel, plan, total_cells), out...  130 us
    dot_general x3, matrix products, over_rows(): lax.dot_general(left, right, (((0,), (0,)), ((), ())), preferred_element_...  71 us
    dot_general x1, matrix products, over_cells(): lax.dot_general(left, right, (((1,), (1,)), ((), ())), preferred_element_...  17.4 us
    dot_general x1, matrix products, rows_dot(): lax.dot_general(left, right, (((1,), (0,)), ((), ())), preferred_element_...  16.4 us
  transfers between devices with their start and end apart: 1, of which 0 were waited for; matrix products, arithmetic and copies ran while one was open for 1% of the time, Pallas kernels for 0%

profile of v3, /device:TPU:11, one launch (start us, length us, event | category | flops | bytes accessed | tf_op | source)
XLA Modules:
  0.0 604.1 jit_solution(3977244328616640409)
XLA Ops:
  0.7 1.0 fusion.20
  1.7 1.0 pad.43
  2.8 2.6 collective-permute-start
  5.4 0.8 copy.43
  6.2 0.8 reshape.56
  8.1 0.9 copy.44
  10.6 1.2 dynamic_slice.26
  14.6 1.0 fusion.17
  15.6 0.9 fusion.54
  16.6 176.9 %shard_map.263 = (bf16[896,7168]{1,0:T(8,128)(2,1)}, bf16[896,3072]{1,0:T(8,128)(2,1)}, bf16[896,7168]{1,0:T(8,128)(2,1)}, f32[100,768]{1,0:T(8,128)}, f32[100,7...) custom-call(bf16[112,1792]{1,0:T(8,128)(2,1)} %get-tuple-element.86., ...), custom_call_target="tpu_custom_call" | custom-call | tf_op jit(solution)/shard_map/pallas_call | solution.py:520
  193.5 19.1 %fusion.7 = f32[7000,768]{1,0:T(8,128)} fusion(bf16[896,7168]{1,0:T(8,128)(2,1)} %get-tuple-element.32, bf16[4,896,768]{2,1,0:T(8,128)(2,1)} %get-tuple-element.33.refs_3_), kind=kOutput, calls=%fused_computation.15 | convolution fusion | flops 9633792000 | bytes 35495936 | tf_op jit(solution)/shard_map/dot_general | solution.py:1183
  212.7 21.5 %multiply_reduce_fusion = (f32[]{:T(128)}, bf16[7000,768]{1,0:T(8,128)(2,1)}, bf16[768,7000]{0,1:T(8,128)(2,1)}, f32[768,7000]{0,1:T(8,128)}) fusion(f32[7000,768]{1,0:T(8,128)} %fusion.7, bf16[768,7000]{0,1:T(8,128)(2,1)S(1)} %bitcast.78, s32[8,7000]{1,0:T(8,128)S(1)} %copy-done.3, s32[768]{0:T(1024)S(1)} %copy-done.4), kind=kOutput, calls=%fused_computation.6 | convolution fusion | flops 123710144 | bytes 75491072 | tf_op jit(solution)/shard_map/dot_general | solution.py:1183
  234.2 16.4 %fusion.5.refs_1_ = f32[896,768]{1,0:T(8,128)} fusion(bf16[7000,768]{1,0:T(8,128)(2,1)} %get-tuple-element.79, bf16[896,7168]{1,0:T(8,128)(2,1)} %get-tuple-element.32), kind=kOutput, calls=%fused_computation.13 | convolution fusion | flops 9633792000 | bytes 26120192 | tf_op jit(solution)/shard_map/dot_general | solution.py:1175
  250.6 17.4 %convolution_convert_fusion = bf16[896,7000]{1,0:T(8,128)(2,1)} fusion(bf16[7000,768]{1,0:T(8,128)(2,1)} %get-tuple-element.79, bf16[4,896,768]{2,1,0:T(8,128)(2,1)} %get-tuple-element.33.refs_3_), kind=kOutput, calls=%fused_computation.12 | convolution fusion | flops 9640064000 | bytes 24672256 | tf_op jit(solution)/shard_map/dot_general | solution.py:1179
  268.0 9.2 %fusion.53 = (bf16[896,1920]{1,0:T(8,128)(2,1)S(1)}, bf16[896,1920]{1,0:T(8,128)(2,1)}, bf16[896,1920]{1,0:T(8,128)(2,1)}, bf16[896,1920]{1,0:T(8,128)(2,1)}) fusion(bf16[896,7000]{1,0:T(8,128)(2,1)} %convolution_convert_fusion), kind=kLoop, calls=%fused_computation.100 | loop fusion | bytes 36700160 | tf_op jit(solution)/shard_map/slice | solution.py:1264
  277.9 1.8 subtract_reduce_fusion
  280.3 10.7 %pad_maximum_fusion.refs_0_ = bf16[896,7680]{1,0:T(8,128)(2,1)} fusion(bf16[896,1920]{1,0:T(8,128)(2,1)} %get-tuple-element.82, bf16[896,1920]{1,0:T(8,128)(2,1)} %get-tuple-element.83, bf16[896,1920]{1,0:T(8,128)(2,1)} %get-tuple-element.84, bf16[896,1920]{1,0:T(8,128)(2,1)S(1)} %get-tuple-element.81), kind=kLoop, calls=%fused_computation.9 | loop fusion | flops 55050240 | bytes 27525120 | tf_op jit(solution)/shard_map/concatenate | solution.py:1263
  291.6 129.9 %shard_map.264 = (f32[112,1920]{1,0:T(8,128)}, f32[4,3,896]{2,1,0:T(4,128)}, bf16[896,3072]{1,0:T(8,128)(2,1)}, bf16[896,768]{1,0:T(8,128)(2,1)}) custom-call(bf16[896,7680]{1,0:T(8,128)(2,1)} %pad_maximum_fusion.refs_0_, f32[896,768]{1,0:T(8,128)} %fusion.5.refs_1_, bf16[896,3072]{1,0:T(8,128)(2,1)} %get-tuple-element.35.refs_2_, ...), custom_call_target="tpu_custom_call" | custom-call | tf_op jit(solution)/shard_map/pallas_call | solution.py:1053
  421.5 1.5 slice.116.refs_3_
  423.0 136.0 %shard_map.265 = (f32[112,1920]{1,0:T(8,128)}, f32[112,768]{1,0:T(8,128)}, f32[1,2048]{1,0:T(1,128)}, f32[112,128]{1,0:T(8,128)}) custom-call(bf16[896,3072]{1,0:T(8,128)(2,1)} %get-tuple-element.44.refs_0_, bf16[7000,768]{1,0:T(8,128)(2,1)} %bitcast.76, bf16[896,768]{1,0:T(8,128)(2,1)} %get-tuple-element.42.refs_2_, f32[1,1920]{1,0:T(1,128)} %slice.116.refs_3_), custom_call_target="tpu_custom_call" | custom-call | tf_op jit(solution)/shard_map/pallas_call | solution.py:1153
  559.0 1.0 fusion.55
  561.5 1.1 slice_bitcast_fusion.9
  567.0 2.7 dynamic-slice_bitcast_fusion
  570.4 30.4 %fusion.2 = bf16[768,7000]{0,1:T(8,128)(2,1)} fusion(f32[768,7000]{0,1:T(8,128)} %get-tuple-element.97, f32[7000,768]{1,0:T(8,128)} %fusion.7, bf16[768,7000]{0,1:T(8,128)(2,1)} %param.16, bf16[896,768]{1,0:T(8,128)(2,1)S(1)} %copy-done.1, bf16[896,7168]{1,0:T(8,128)(2,1)} %get-tuple-element.43), kind=kOutput, calls=%fused_computation.5 | convolution fusion | flops 9660672000 | bytes 78503936 | tf_op jit(solution)/shard_map/dot_general | solution.py:1183
  (51 shorter events, 12.1 us)
Async XLA Ops:
  2.8 11.9 %collective-permute-start = (bf16[224,256]{1,0:T(8,128)(2,1)S(1)}, bf16[224,256]{1,0:T(8,128)(2,1)S(1)}, u32[]{:S(2)}, u32[]{:S(2)}) collective-permute-start(bf16[224,256]{1,0:T(8,128)(2,1)S(1)} %pad_maximum_fusion.1), channel_id=1, source_target_pairs={{1,0},{2,1},{3,2},{5,4},{6,5},{7,6},{9,8},{10,9},{11,10},{13,12},{... | collective-permute-start | bytes 344072 | tf_op jit(solution)/shard_map/ppermute | solution.py:1233
  16.6 196.1 %slice-start = ((s8[10752000]{0:T(1024)(128)(4,1)}), s8[2363392]{0:T(1024)(128)(4,1)S(1)}, s32[]{:S(2)}) async-start(s8[10752000]{0:T(1024)(128)(4,1)} %bitcast.77), calls=%async_computation | async-start | bytes 4726784
  193.5 19.2 %slice-start.1 = ((s8[10752000]{0:T(1024)(128)(4,1)}), s8[4194304]{0:T(1024)(128)(4,1)S(1)}, s32[]{:S(2)}) async-start(s8[10752000]{0:T(1024)(128)(4,1)} %bitcast.77), calls=%async_computation.1 | async-start | bytes 8388608
  193.5 19.2 %slice-start.2 = ((s8[10752000]{0:T(1024)(128)(4,1)}), s8[4194304]{0:T(1024)(128)(4,1)S(1)}, s32[]{:S(2)}) async-start(s8[10752000]{0:T(1024)(128)(4,1)} %bitcast.77), calls=%async_computation.2 | async-start | bytes 8388608
  193.5 19.2 %copy-start.3 = (s32[8,7000]{1,0:T(8,128)S(1)}, s32[8,7000]{1,0:T(8,128)}, u32[]{:S(2)}) copy-start(s32[8,7000]{1,0:T(8,128)} %param.18) | copy-start | bytes 672004
  193.5 19.1 %copy-start.4 = (s32[768]{0:T(1024)S(1)}, s32[768]{0:T(1024)}, u32[]{:S(2)}) copy-start(s32[768]{0:T(1024)} %param.17) | copy-start | bytes 9220
  421.5 141.2 %copy-start.5 = (f32[4,3,896]{2,1,0:T(4,128)S(1)}, f32[4,3,896]{2,1,0:T(4,128)}, u32[]{:S(2)}) copy-start(f32[4,3,896]{2,1,0:T(4,128)} %get-tuple-element.41) | copy-start | bytes 129028
  421.5 145.5 %copy-start.2 = (f32[112,1920]{1,0:T(8,128)S(1)}, f32[112,1920]{1,0:T(8,128)}, u32[]{:S(2)}) copy-start(f32[112,1920]{1,0:T(8,128)} %get-tuple-element.45) | copy-start | bytes 2580484
  423.0 147.4 %copy-start.1 = (bf16[896,768]{1,0:T(8,128)(2,1)S(1)}, bf16[896,768]{1,0:T(8,128)(2,1)}, u32[]{:S(2)}) copy-start(bf16[896,768]{1,0:T(8,128)(2,1)} %get-tuple-element.42.refs_2_) | copy-start | bytes 4128772
  570.4 31.7 %copy-start = (f32[100,768]{1,0:T(8,128)S(1)}, f32[100,768]{1,0:T(8,128)}, u32[]{:S(2)}) copy-start(f32[100,768]{1,0:T(8,128)} %get-tuple-element.34.refs_9_) | copy-start | bytes 921604
